TPU v7x, 256 devices: a whole 4x4x8 slice. The times are simulated.
256 devices in a mesh: section: 16 (over z_hi, x), inner: 16 (over z_lo, y, core).
Axes of the slice: x: 4, y: 4, z: 8 (z_hi: 4, z_lo: 2; z = z_hi * 2 + z_lo), core: 2. Of those that a mesh axis runs over, the one named last changes fastest.
Arguments:
- wavefunction: float32 [256, 64, 1024], P(('section', 'inner'))
- environments: bfloat16 [512, 34, 4096], P(('section', 'inner')), as said below
- mpo_terms: bfloat16 [34, 16, 16], replicated, as said below
- sector_dims: int32 [256, 2], P(('section', 'inner')), may hold values from 32 to 64, as said below
- channel_charges: int32 [34], replicated, may hold values from -1 to 1, as said below
Outputs:
- optimized: float32 [256, 64, 1024], P(('section', 'inner'))
- energy: float32 [16], P('section')
Inputs may be any that keep to these rules, and one draw needn't show every extreme that they name: Each 64 x 64 matrix of environments is symmetric. Each 16 x 16 matrix of mpo_terms is symmetric. `sector_dims`: at least one block has 64 live states on both sides. `channel_charges`: both -1 and 1 occur among the channels.
All inputs are finite; a program needn't handle non-finite values.
Results may differ from a plain program's by a relative error of at most 0.02.
Values may be sent and summed in bfloat16 or wider, within the bound.
A program may use at most 128 MiB of HBM per device.

v0:
```python
import jax
import jax.numpy as jnp
from jax import lax
from jax.sharding import PartitionSpec as P

ITERS = 2


EPSILON = 1e-06


def with_halo(value, sides, width):
    for axis, dim in sides:
        size, length = (lax.axis_size(axis), value.shape[dim])
        up = [(i, (i + 1) % size) for i in range(size)]
        down = [(j, i) for i, j in up]
        last = lax.slice_in_dim(value, length - width, length, axis=dim)
        first = lax.slice_in_dim(value, 0, width, axis=dim)
        before = lax.ppermute(last, axis, up)
        after = lax.ppermute(first, axis, down)
        value = jnp.concatenate([before, value, after], axis=dim)
    return value


def swapped(block, axis, distance):
    count = lax.axis_size(axis)
    route = []
    for low in range(count):
        high = low | 1 << distance
        if high != low and high < count:
            route += [(low, high), (high, low)]
    return lax.ppermute(block, axis, route)


def build_mask(dims, block_rows, row_width):
    rows = jnp.arange(block_rows)[None, :, None]
    cols = (jnp.arange(row_width) % block_rows)[None, None, :]
    live = (rows < dims[:, 0][:, None, None]) & (cols < dims[:, 1][:, None, None])
    return live.astype(jnp.float32)


def neighbour_fields(lowered):
    blocks = lowered.shape[0]
    padded = with_halo(lowered, (("inner", 0),), blocks)
    below = padded[:blocks]
    above = padded[2 * blocks :]
    return (below, above)


def apply_operator(vector, left, right, mpo_terms, mask, channel_charges):
    blocks = vector.shape[0]
    block_rows = vector.shape[1]
    channels = left.shape[1]
    states = mpo_terms.shape[1]
    lowered = vector.astype(jnp.bfloat16)
    below, above = neighbour_fields(lowered)
    stacked = jnp.stack([below, lowered, above])
    sources = jnp.take(stacked, channel_charges + 1, axis=0)
    left_mat = left.reshape(blocks, channels, block_rows, block_rows)
    first = jnp.einsum(
        "kalm,akmn->kaln", left_mat, sources, preferred_element_type=jnp.float32
    ).astype(jnp.bfloat16)
    first = first.reshape(blocks, channels, block_rows, states, block_rows)
    mixed = jnp.einsum(
        "kalsr,ast->kaltr", first, mpo_terms, preferred_element_type=jnp.float32
    ).astype(jnp.bfloat16)
    right_mat = right.reshape(blocks, channels, block_rows, block_rows)
    image = jnp.einsum("kaltr,kaqr->kltq", mixed, right_mat, preferred_element_type=jnp.float32)
    return image.reshape(blocks, block_rows, states * block_rows) * mask


def pair_total(values):
    stacked = jnp.stack(values)
    slot = lax.axis_index("section") // 2
    boundaries = lax.axis_size("section") // 2
    selector = (jnp.arange(boundaries) == slot).astype(jnp.float32)
    table = selector[:, None] * stacked[None, :]
    summed = lax.psum(table, ("section", "inner"))
    totals = jnp.sum(selector[:, None] * summed, axis=0)
    return totals


def rotation_terms(energy_now, coupling, curvature):
    angle = 0.5 * jnp.arctan2(-coupling, 0.5 * (curvature - energy_now))
    lowest = 0.5 * (energy_now + curvature) - jnp.sqrt(
        0.25 * (energy_now - curvature) ** 2 + coupling**2
    )
    return (jnp.cos(angle), jnp.sin(angle), lowest)


def body(wavefunction, environments, mpo_terms, sector_dims, channel_charges):
    own_blocks = wavefunction.shape[0]
    block_rows = wavefunction.shape[1]
    row_width = wavefunction.shape[2]
    parity = lax.axis_index("section") % 2
    even_side = parity == 0
    entries = 1.0 * lax.axis_size("inner") * 2 * own_blocks * block_rows * row_width
    outgoing = lax.dynamic_slice_in_dim(environments, (1 - parity) * own_blocks, own_blocks, 0)
    kept = lax.dynamic_slice_in_dim(environments, parity * own_blocks, own_blocks, 0)
    arrived = swapped(outgoing, "section", 0)
    left = jnp.where(even_side, kept, arrived)
    right = jnp.where(even_side, arrived, kept)
    mask = build_mask(sector_dims, block_rows, row_width)
    start = wavefunction * mask
    norm_start = pair_total([jnp.sum(start * start)])[0] / entries
    psi = start / jnp.sqrt(norm_start + EPSILON)
    image = apply_operator(psi, left, right, mpo_terms, mask, channel_charges)
    energy_now = pair_total([jnp.sum(psi * image)])[0] / entries
    lowest = energy_now
    for iteration in range(ITERS):
        resid = image - energy_now * psi
        resid_norm = pair_total([jnp.sum(resid * resid)])[0] / entries
        direction = resid / jnp.sqrt(resid_norm + EPSILON)
        turned = apply_operator(direction, left, right, mpo_terms, mask, channel_charges)
        pieces = pair_total([jnp.sum(direction * image), jnp.sum(direction * turned)]) / entries
        cosine, sine, lowest = rotation_terms(energy_now, pieces[0], pieces[1])
        psi = cosine * psi + sine * direction
        image = cosine * image + sine * turned
        energy_now = pair_total([jnp.sum(psi * image)])[0] / entries
    return (psi, jnp.reshape(lowest, (1,)))


def solution(mesh):
    return jax.shard_map(
        body,
        mesh=mesh,
        in_specs=(
            P(("section", "inner"), None, None),
            P(("section", "inner"), None, None),
            P(),
            P(("section", "inner"), None),
            P(),
        ),
        out_specs=(P(("section", "inner"), None, None), P("section")),
        check_vma=False,
    )
```

profile of v0, /device:TPU:1, one launch (start us, length us, event | category | flops | bytes accessed | tf_op | source)
XLA Modules:
  0.0 681.1 jit_solution(6951792043967387327)
XLA Ops:
  0.6 1.3 fusion.56
  2.0 0.7 fusion.39
  2.6 0.7 iota_compare_fusion.1
  3.3 1.7 multiply_reduce_fusion.7
  5.0 0.6 fusion.47
  5.6 81.4 %psum.49 = f32[8,1]{0,1:T(1,128)S(1)} all-reduce(f32[8,1]{0,1:T(1,128)S(1)} %fusion.47), channel_id=1, replica_groups=mesh['section'=16,'inner'=16] {'section','inner'}, use_global_device_ids=true, to_apply=%region_1.2 | all-reduce | flops 8 | bytes 64 | tf_op jit(solution)/shard_map/psum | solution.py:78
  87.1 0.6 select_reduce_fusion.4
  88.3 1.1 fusion.53
  89.5 1.0 collective-permute-start.2
  90.6 2.5 constant_dynamic-slice_fusion.1
  93.1 0.3 copy.57
  93.4 0.6 collective-permute-start
  94.0 1.1 fusion.69
  95.0 0.7 compare_and_fusion
  95.7 1.1 copy.44
  96.8 4.3 gather_fusion
  101.1 0.3 broadcast_select_fusion.1
  101.4 0.6 reshape.455
  102.1 5.8 fusion.15
  107.8 12.4 %reshape.457 = bf16[34,64,16,64]{3,2,1,0:T(8,128)(2,1)} reshape(bf16[34,64,1024]{2,1,0:T(8,128)(2,1)} %fusion.15) | data formatting | bytes 8912896 | tf_op jit(solution)/shard_map/reshape.9
  120.2 0.6 reshape.516
  120.8 6.0 convert_bitcast_fusion.2
  126.8 2.5 fusion.27
  129.8 0.8 multiply_reduce_fusion.6
  130.5 0.6 fusion.46
  131.2 76.6 %psum.50 = f32[8,1]{0,1:T(1,128)S(1)} all-reduce(f32[8,1]{0,1:T(1,128)S(1)} %fusion.46), channel_id=1, replica_groups=mesh['section'=16,'inner'=16] {'section','inner'}, use_global_device_ids=true, to_apply=%region_4.6 | all-reduce | flops 8 | bytes 64 | tf_op jit(solution)/shard_map/psum | solution.py:78
  207.8 0.6 select_reduce_fusion.3
  209.0 0.8 multiply_reduce_fusion.5
  209.8 0.6 fusion.45
  210.5 73.7 %psum.51 = f32[8,1]{0,1:T(1,128)S(1)} all-reduce(f32[8,1]{0,1:T(1,128)S(1)} %fusion.45), channel_id=1, replica_groups=mesh['section'=16,'inner'=16] {'section','inner'}, use_global_device_ids=true, to_apply=%region_7.9 | all-reduce | flops 8 | bytes 64 | tf_op jit(solution)/shard_map/psum | solution.py:78
  284.2 0.6 select_reduce_fusion.2
  285.6 1.5 collective-permute-start.3
  287.2 1.9 collective-permute-done.3
  289.1 2.7 collective-permute-done.4
  291.9 4.3 gather_fusion.1
  296.2 5.8 fusion.18
  301.9 12.4 %reshape.462 = bf16[34,64,16,64]{3,2,1,0:T(8,128)(2,1)} reshape(bf16[34,64,1024]{2,1,0:T(8,128)(2,1)} %fusion.18) | data formatting | bytes 8912896 | tf_op jit(solution)/shard_map/reshape.36
  314.3 6.0 convert_bitcast_fusion.1
  320.3 2.5 fusion.30
  323.3 0.8 multiply_reduce_fusion.4
  324.1 1.4 pad_maximum_fusion
  325.5 77.2 %psum.52 = f32[8,2]{0,1:T(2,128)S(1)} all-reduce(f32[8,2]{0,1:T(2,128)S(1)} %broadcast_multiply_fusion.1), channel_id=1, replica_groups=mesh['section'=16,'inner'=16] {'section','inner'}, use_global_device_ids=true, to_apply=%region_11.13 | all-reduce | flops 16 | bytes 128 | tf_op jit(solution)/shard_map/psum | solution.py:78
  402.8 0.6 fusion.55
  405.0 0.8 multiply_reduce_fusion.2
  405.8 0.6 fusion.44
  406.4 73.2 %psum.53 = f32[8,1]{0,1:T(1,128)S(1)} all-reduce(f32[8,1]{0,1:T(1,128)S(1)} %fusion.44), channel_id=1, replica_groups=mesh['section'=16,'inner'=16] {'section','inner'}, use_global_device_ids=true, to_apply=%region_14.16 | all-reduce | flops 8 | bytes 64 | tf_op jit(solution)/shard_map/psum | solution.py:78
  479.6 0.6 select_reduce_fusion.1
  480.8 0.7 multiply_reduce_fusion.1
  481.5 0.6 fusion.43
  482.2 73.3 %psum.54 = f32[8,1]{0,1:T(1,128)S(1)} all-reduce(f32[8,1]{0,1:T(1,128)S(1)} %fusion.43), channel_id=1, replica_groups=mesh['section'=16,'inner'=16] {'section','inner'}, use_global_device_ids=true, to_apply=%region_17.19 | all-reduce | flops 8 | bytes 64 | tf_op jit(solution)/shard_map/psum | solution.py:78
  555.4 0.6 select_reduce_fusion
  556.8 1.3 collective-permute-start.5
  558.1 1.9 collective-permute-done.5
  560.0 2.7 collective-permute-done.6
  562.8 4.3 gather_fusion.2
  567.1 5.8 fusion.21
  572.9 12.4 %reshape.466 = bf16[34,64,16,64]{3,2,1,0:T(8,128)(2,1)} reshape(bf16[34,64,1024]{2,1,0:T(8,128)(2,1)} %fusion.21) | data formatting | bytes 8912896 | tf_op jit(solution)/shard_map/reshape.48
  585.2 6.0 convert_bitcast_fusion
  591.2 2.5 fusion.33
  594.2 0.8 multiply_reduce_fusion
  594.9 1.4 pad_maximum_fusion.1
  596.4 77.8 %psum.55 = f32[8,2]{0,1:T(2,128)S(1)} all-reduce(f32[8,2]{0,1:T(2,128)S(1)} %broadcast_multiply_fusion), channel_id=1, replica_groups=mesh['section'=16,'inner'=16] {'section','inner'}, use_global_device_ids=true, to_apply=%region_21.23 | all-reduce | flops 16 | bytes 128 | tf_op jit(solution)/shard_map/psum | solution.py:78
  674.3 0.6 fusion.54
  679.0 0.8 multiply_add_fusion
  (27 shorter events, 2.3 us)
Async XLA Ops:
  89.4 7.3 %collective-permute-start.1 = (bf16[1,64,1024]{2,1,0:T(8,128)(2,1)S(1)}, bf16[1,64,1024]{2,1,0:T(8,128)(2,1)S(1)}, u32[]{:S(2)}, u32[]{:S(2)}) collective-permute-start(bf16[1,64,1024]{2,1,0:T(8,128)(2,1)S(1)} %fusion.53), channel_id=1, source_target_pairs={{0,1},{1,2},{2,3},{3,4},{4,5},{5,6},{6,7},{7,8},{8,9},{9,10},{10,1... | collective-permute-start | bytes 393224 | tf_op jit(solution)/shard_map/ppermute | solution.py:19
  89.5 7.3 %collective-permute-start.2 = (bf16[1,64,1024]{2,1,0:T(8,128)(2,1)S(1)}, bf16[1,64,1024]{2,1,0:T(8,128)(2,1)S(1)}, u32[]{:S(2)}, u32[]{:S(2)}) collective-permute-start(bf16[1,64,1024]{2,1,0:T(8,128)(2,1)S(1)} %fusion.53), channel_id=1, source_target_pairs={{1,0},{2,1},{3,2},{4,3},{5,4},{6,5},{7,6},{8,7},{9,8},{10,9},{11,1... | collective-permute-start | bytes 393224 | tf_op jit(solution)/shard_map/ppermute | solution.py:20
  93.4 7.7 %collective-permute-start = (bf16[1,34,4096]{2,1,0:T(8,128)(2,1)S(1)}, bf16[1,34,4096]{2,1,0:T(8,128)(2,1)S(1)}, u32[]{:S(2)}, u32[]{:S(2)}) collective-permute-start(bf16[1,34,4096]{2,1,0:T(8,128)(2,1)S(1)} %copy.57), channel_id=1, source_target_pairs={{0,16},{16,0},{32,48},{48,32},{64,80},{80,64},{96,112},{112,96},{1... | collective-permute-start | bytes 835592 | tf_op jit(solution)/shard_map/ppermute | solution.py:32
  126.8 3.0 copy-start
  285.6 3.5 collective-permute-start.3
  287.2 4.7 collective-permute-start.4
  556.8 3.3 collective-permute-start.5
  558.1 4.7 collective-permute-start.6
where the time goes:
time: 687 us; the launch traced here: 681 us
  blocking collectives  533 us (78%)
  local copies, waits for them, and re-layouts  59 us (9%)
  matrix products  42.6 us (6%)
  other arithmetic  21.2 us (3%)
  between operations  11.3 us (2%)
  waiting for transfers between devices  9.37 us (1%)
    psum x7, blocking collectives, pair_total(): summed = lax.psum(table, ('section', 'inner'))  533 us
    another operation x5, local copies, waits for them, and re-layouts  38.4 us
    dot_general x3, matrix products, apply_operator(): jnp.einsum('kalsr,ast->kaltr', first, mpo_terms, preferred_element_type=j...  17.9 us
    dot_general x3, matrix products, apply_operator(): jnp.einsum('kalm,akmn->kaln', left_mat, sources, preferred_element_type=j...  17.3 us
  transfers between devices with their start and end apart: 7, of which 4 were waited for; matrix products, arithmetic and copies ran while one was open for 1% of the time, Pallas kernels for 0%

commit v1 on v0

v1 whole, which is shorter than its diff:
```python
import functools

import jax
import jax.numpy as jnp
from jax import lax
from jax.experimental import pallas as pl
from jax.experimental.pallas import tpu as pltpu
from jax.sharding import PartitionSpec as P

MESH = pl.DeviceIdType.MESH
F32 = jnp.float32
BF16 = jnp.bfloat16

ITERS = 2
EPSILON = 1e-06
BLK = 64
CHAN = 34
PH = 16
WIDTH = PH * BLK
HALF = CHAN // 2

GROUPS = (
    tuple((0, d) for d in range(8)),
    ((0, 0), (0, 8), (1, 0), (1, 8)),
)
SLOTS = sum(len(group) for group in GROUPS)


def flipped(index, bits):
    for bit in (1, 2, 4, 8):
        if bits & bit:
            index = index + bit * (1 - 2 * ((index // bit) % 2))
    return index


def low_half(rows):
    return lax.broadcasted_iota(jnp.int32, (rows, 128), 1) < BLK


def interchange(a, b, low):
    turned_a = pltpu.roll(a, BLK, 1)
    turned_b = pltpu.roll(b, BLK, 1)
    return jnp.where(low, a, turned_b), jnp.where(low, turned_a, b)


def to_mixed(field):
    low = low_half(16)
    rows = []
    for j in range(PH // 2):
        even, odd = [], []
        for p in range(2):
            a = field[32 * p : 32 * p + 16, 128 * j : 128 * j + 128]
            b = field[32 * p + 16 : 32 * p + 32, 128 * j : 128 * j + 128]
            first, second = interchange(a, b, low)
            even.append(first)
            odd.append(second)
        rows.append(jnp.concatenate(even, axis=1))
        rows.append(jnp.concatenate(odd, axis=1))
    return rows


def kernel(
    wave_ref, env_ref, mpo_ref, dims_ref, charge_ref, psi_ref, energy_ref,
    raw, wide, lsel, rsel, wsel, first, fields, image, sources,
    halo, mask, start_buf, vec_im, vec_q, vec_t, exchange,
    env_send, env_recv, halo_send, halo_recv, red_send, red_recv,
):
    section, inner = lax.axis_index("section"), lax.axis_index("inner")
    n_inner = lax.axis_size("inner")
    parity = section % 2
    entries = 2.0 * n_inner * BLK * WIDTH

    def at(h, d):
        return (flipped(section, h), flipped(inner, d))

    above = (section, (inner + 1) % n_inner)
    below = (section, (inner + n_inner - 1) % n_inner)
    partner = at(1, 0)

    peers = [at(h, d) for group in GROUPS for h, d in group[1:]] + [above, below, partner]
    barrier = pltpu.get_barrier_semaphore()
    for peer in peers:
        pl.semaphore_signal(barrier, inc=1, device_id=peer, device_id_type=MESH)

    kept = pltpu.make_async_copy(env_ref.at[parity], raw.at[parity], env_recv.at[parity])
    kept.start()

    def dot_rows(pairs):
        rows = []
        for x, y in pairs:
            prod = x * y
            tot = None
            for i in range(BLK // 8):
                for j in range(WIDTH // 128):
                    tile = prod[8 * i : 8 * i + 8, 128 * j : 128 * j + 128]
                    tot = tile if tot is None else tot + tile
            rows.append(jnp.sum(tot, axis=0, keepdims=True))
        rows.append(jnp.zeros((8 - len(rows), 128), F32))
        return jnp.concatenate(rows, axis=0)

    def red_base(phase):
        return sum(len(group) for group in GROUPS[:phase])

    def red_start(slot, phase, value):
        base = red_base(phase)
        exchange[slot, base] = value
        for j, (h, d) in enumerate(GROUPS[phase][1:]):
            pltpu.make_async_remote_copy(
                src_ref=exchange.at[slot, base],
                dst_ref=exchange.at[slot, base + 1 + j],
                send_sem=red_send.at[slot, phase],
                recv_sem=red_recv.at[slot, phase],
                device_id=at(h, d),
                device_id_type=MESH,
            ).start()

    def red_finish(slot, phase):
        base, count = red_base(phase), len(GROUPS[phase])
        arrived = exchange.at[slot, pl.ds(base + 1, count - 1)]
        pltpu.make_async_copy(arrived, arrived, red_recv.at[slot, phase]).wait()
        parts = [exchange[slot, base + j] for j in range(count)]
        while len(parts) > 1:
            parts = [parts[2 * k] + parts[2 * k + 1] for k in range(len(parts) // 2)]
        return parts[0]

    def red_total(slot):
        value = red_finish(slot, 0)
        for phase in range(1, len(GROUPS)):
            red_start(slot, phase, value)
            value = red_finish(slot, phase)
        return jnp.sum(value, axis=1, keepdims=True) * (1.0 / entries)

    def red_drain(slot):
        for phase in range(len(GROUPS)):
            base, count = red_base(phase), len(GROUPS[phase])
            sent = exchange.at[slot, pl.ds(base + 1, count - 1)]
            pltpu.make_async_copy(sent, sent, red_send.at[slot, phase]).wait()

    def halo_copies(k):
        return [
            pltpu.make_async_remote_copy(
                src_ref=halo.at[k, 1],
                dst_ref=halo.at[k, 2 * side],
                send_sem=halo_send.at[k, side],
                recv_sem=halo_recv.at[k, side],
                device_id=target,
                device_id_type=MESH,
            )
            for side, target in ((0, above), (1, below))
        ]

    def apply():
        def left_step(c, _):
            rows = pl.ds(pl.multiple_of(c * (HALF * BLK), HALF * BLK), HALF * BLK)
            out = jnp.dot(lsel[rows, :], sources[...], preferred_element_type=F32).astype(BF16)
            for k in range(HALF):
                parts = to_mixed(out[k * BLK : (k + 1) * BLK])
                for s in range(PH):
                    first[c * HALF + k, 16 * s : 16 * s + 16, :] = parts[s]
            return 0

        lax.fori_loop(0, 2, left_step, 0)

        image[...] = jnp.zeros_like(image)

        def right_step(c, _):
            mixed = [
                jnp.dot(wsel[c * HALF + k], first[c * HALF + k], preferred_element_type=F32).astype(BF16)
                for k in range(HALF)
            ]
            right = rsel[pl.ds(c * HALF, HALF)].reshape(HALF * 256, 256)
            image[...] += jnp.dot(jnp.concatenate(mixed, axis=1), right, preferred_element_type=F32)
            return 0

        lax.fori_loop(0, 2, right_step, 0)

        low = low_half(16)
        for j in range(PH // 2):
            for p in range(2):
                a = image[32 * j : 32 * j + 16, 128 * p : 128 * p + 128]
                b = image[32 * j + 16 : 32 * j + 32, 128 * p : 128 * p + 128]
                upper, lower = interchange(a, b, low)
                lanes = slice(128 * j, 128 * j + 128)
                vec_t[32 * p : 32 * p + 16, lanes] = upper * mask[32 * p : 32 * p + 16, :]
                vec_t[32 * p + 16 : 32 * p + 32, lanes] = lower * mask[32 * p + 16 : 32 * p + 32, :]

    def scalar(total, k):
        return total[k : k + 1, :]

    row = lax.broadcasted_iota(jnp.int32, (BLK, 128), 0)
    lane = lax.broadcasted_iota(jnp.int32, (BLK, 128), 1)
    live = (row < dims_ref[0, 0]) & (lane % BLK < dims_ref[0, 1])
    mask[...] = jnp.where(live, 1.0, 0.0).astype(F32)
    start = wave_ref[0] * jnp.concatenate([mask[...]] * (WIDTH // 128), axis=1)
    start_buf[...] = start
    halo[0, 1] = start.astype(BF16)
    norm_rows = dot_rows([(start, start)])

    pl.semaphore_wait(barrier, len(peers))
    outgoing = pltpu.make_async_remote_copy(
        src_ref=env_ref.at[1 - parity],
        dst_ref=raw.at[parity],
        send_sem=env_send,
        recv_sem=env_recv.at[parity],
        device_id=partner,
        device_id_type=MESH,
    )
    outgoing.start()
    start_halo = halo_copies(0)
    for copy in start_halo:
        copy.start()
    red_start(0, 0, norm_rows)

    spread = (
        lax.broadcasted_iota(jnp.int32, (PH, 256), 1) // 16 == lax.broadcasted_iota(jnp.int32, (PH, 256), 0)
    ).astype(BF16)
    spread_rows = (
        lax.broadcasted_iota(jnp.int32, (256, PH), 0) // 16 == lax.broadcasted_iota(jnp.int32, (256, PH), 1)
    ).astype(BF16)
    same = (
        lax.broadcasted_iota(jnp.int32, (256, 256), 0) % 16 == lax.broadcasted_iota(jnp.int32, (256, 256), 1) % 16
    )

    def mpo_step(c, _):
        for k in range(HALF):
            a = c * HALF + k
            lanes = jnp.dot(mpo_ref[a], spread, preferred_element_type=F32).astype(BF16)
            both = jnp.dot(spread_rows, lanes, preferred_element_type=F32)
            wsel[a] = jnp.where(same, both, 0.0).astype(BF16)
        return 0

    lax.fori_loop(0, 2, mpo_step, 0)

    def unfold(slot):
        for j in range(BLK // 2):
            pair = raw[slot, :, 128 * j : 128 * j + 128].astype(F32)
            wide[slot, pl.ds(2 * j, CHAN, stride=BLK), :] = pair
            wide[slot, pl.ds(2 * j + 1, CHAN, stride=BLK), :] = pair

    own = (row % 2 == 0) == (lane < BLK)

    def doubled(slot, a):
        x = wide[slot, pl.ds(pl.multiple_of(a * BLK, BLK), BLK), :]
        return jnp.where(own, x, pltpu.roll(x, BLK, 1))

    kept.wait()
    unfold(parity)
    arrived = raw.at[1 - parity]
    pltpu.make_async_copy(arrived, arrived, env_recv.at[1 - parity]).wait()
    unfold(1 - parity)

    low64 = lane < BLK

    def env_step(c, _):
        for k in range(HALF):
            a = c * HALF + k
            charge = charge_ref[a]
            rows = pl.ds(pl.multiple_of(a * BLK, BLK), BLK)
            left = doubled(0, a)
            wanted = jnp.where(low64, -1, 0)
            lsel[rows, 0:128] = jnp.where(wanted == charge, left, 0.0).astype(BF16)
            lsel[rows, 128:192] = jnp.where(low64 & (charge == 1), left, 0.0).astype(BF16)[:, :BLK]
            right = doubled(1, a).astype(BF16)
            zero = jnp.zeros((2 * BLK, 128), BF16)
            block = jnp.concatenate(
                [jnp.where(low64, right, jnp.zeros_like(right)), jnp.where(low64, jnp.zeros_like(right), right)], axis=0
            )
            rsel[a, 0:128, 0:128] = block
            rsel[a, 128:256, 128:256] = block
            rsel[a, 0:128, 128:256] = zero
            rsel[a, 128:256, 0:128] = zero
        return 0

    lax.fori_loop(0, 2, env_step, 0)

    for copy in start_halo:
        copy.wait_recv()
    for k in range(3):
        sources[k * BLK : (k + 1) * BLK, :] = halo[0, k]
    norm = scalar(red_total(0), 0)
    scale = 1.0 / jnp.sqrt(norm + EPSILON)
    apply()
    im = vec_t[...] * scale
    vec_im[...] = im
    halo[1, 1] = im.astype(BF16)
    halos = [halo_copies(1), halo_copies(2)]
    for copy in halos[0]:
        copy.start()
    psi = start_buf[...] * scale
    start_buf[...] = psi
    red_start(1, 0, dot_rows([(psi, im), (im, im)]))
    totals = red_total(1)
    energy_now = scalar(totals, 0)
    unit = jnp.sqrt(scalar(totals, 1) + EPSILON)
    inverse = 1.0 / unit

    vec_q[...] = (vec_im[...] - energy_now * start_buf[...]) * inverse
    for copy in halos[0]:
        copy.wait_recv()
    sources[BLK : 2 * BLK, :] = vec_q[...].astype(BF16)
    for k in (0, 2):
        field = (halo[1, k].astype(F32) - (energy_now * scale) * halo[0, k].astype(F32)) * inverse
        sources[k * BLK : (k + 1) * BLK, :] = field.astype(BF16)
    apply()
    halo[2, 1] = vec_t[...].astype(BF16)
    for copy in halos[1]:
        copy.start()
    q, t, psi, im = vec_q[...], vec_t[...], start_buf[...], vec_im[...]
    red_drain(0)
    red_start(0, 0, dot_rows([(q, q), (q, im), (q, t), (psi, t)]))
    totals = red_total(0)

    def rotation(energy, coupling, curvature):
        x = 0.5 * (curvature - energy)
        size = jnp.maximum(jnp.abs(x), jnp.abs(coupling))
        safe = jnp.where(size > 0.0, size, 1.0)
        xs, ys = x / safe, -coupling / safe
        radius = jnp.sqrt(xs * xs + ys * ys)
        radius = jnp.where(size > 0.0, radius, 1.0)
        cos2 = jnp.where(size > 0.0, xs / radius, 1.0)
        sin2 = ys / radius
        big = jnp.sqrt(0.5 + 0.5 * jnp.abs(cos2))
        small = 0.5 * sin2 / big
        sign = jnp.where(coupling < 0.0, 1.0, -1.0)
        cosine = jnp.where(cos2 >= 0.0, big, jnp.abs(small))
        sine = jnp.where(cos2 >= 0.0, small, sign * big)
        lowest = 0.5 * (energy + curvature) - jnp.sqrt(x * x + coupling * coupling)
        return cosine, sine, lowest

    def kappa_of(square):
        return unit / jnp.sqrt(unit * unit * square + EPSILON)

    kappa = kappa_of(scalar(totals, 0))
    coupling = kappa * scalar(totals, 1)
    curvature = kappa * kappa * scalar(totals, 2)
    mirrored = kappa * scalar(totals, 3)
    cosine, sine, _ = rotation(energy_now, coupling, curvature)
    energy_next = (
        cosine * cosine * energy_now + cosine * sine * (coupling + mirrored) + sine * sine * curvature
    )
    turn = sine * kappa
    psi = cosine * start_buf[...] + turn * vec_q[...]
    im = cosine * vec_im[...] + turn * vec_t[...]
    start_buf[...] = psi
    vec_im[...] = im
    q = (im - energy_next * psi) * inverse
    vec_q[...] = q
    sources[BLK : 2 * BLK, :] = q.astype(BF16)

    for copy in halos[1]:
        copy.wait_recv()
    for k in (0, 2):
        h_psi = halo[0, k].astype(F32) * scale
        h_im = halo[1, k].astype(F32)
        h_q = (h_im - energy_now * h_psi) * inverse
        n_psi = cosine * h_psi + turn * h_q
        n_im = cosine * h_im + turn * halo[2, k].astype(F32)
        sources[k * BLK : (k + 1) * BLK, :] = ((n_im - energy_next * n_psi) * inverse).astype(BF16)
    apply()
    q, t, im = vec_q[...], vec_t[...], vec_im[...]
    red_drain(1)
    red_start(1, 0, dot_rows([(q, q), (q, im), (q, t)]))
    totals = red_total(1)
    kappa = kappa_of(scalar(totals, 0))
    coupling = kappa * scalar(totals, 1)
    curvature = kappa * kappa * scalar(totals, 2)
    cosine, sine, lowest = rotation(energy_next, coupling, curvature)
    psi_ref[0] = cosine * start_buf[...] + (sine * kappa) * vec_q[...]
    energy_ref[...] = jnp.broadcast_to(lowest, (1, 128))

    red_drain(0)
    red_drain(1)
    outgoing.wait_send()
    for copies in [start_halo] + halos:
        for copy in copies:
            copy.wait_send()


def body(wavefunction, environments, mpo_terms, sector_dims, channel_charges):
    vmem = pl.BlockSpec(memory_space=pltpu.VMEM)
    smem = pl.BlockSpec(memory_space=pltpu.SMEM)
    psi, energy = pl.pallas_call(
        kernel,
        out_shape=(
            jax.ShapeDtypeStruct((1, BLK, WIDTH), F32),
            jax.ShapeDtypeStruct((1, 128), F32),
        ),
        in_specs=[vmem, pl.BlockSpec(memory_space=pl.ANY), vmem, smem, smem],
        out_specs=(vmem, vmem),
        scratch_shapes=[
            pltpu.VMEM((2, CHAN, BLK * BLK), BF16),
            pltpu.VMEM((2, CHAN * BLK, 128), F32),
            pltpu.VMEM((CHAN * BLK, 3 * BLK), BF16),
            pltpu.VMEM((CHAN, 256, 256), BF16),
            pltpu.VMEM((CHAN, 256, 256), BF16),
            pltpu.VMEM((CHAN, 256, 256), BF16),
            pltpu.VMEM((8, 128), F32),
            pltpu.VMEM((256, 256), F32),
            pltpu.VMEM((3 * BLK, WIDTH), BF16),
            pltpu.VMEM((3, 3, BLK, WIDTH), BF16),
            pltpu.VMEM((BLK, 128), F32),
            pltpu.VMEM((BLK, WIDTH), F32),
            pltpu.VMEM((BLK, WIDTH), F32),
            pltpu.VMEM((BLK, WIDTH), F32),
            pltpu.VMEM((BLK, WIDTH), F32),
            pltpu.VMEM((2, SLOTS, 8, 128), F32),
            pltpu.SemaphoreType.DMA,
            pltpu.SemaphoreType.DMA((2,)),
            pltpu.SemaphoreType.DMA((3, 2)),
            pltpu.SemaphoreType.DMA((3, 2)),
            pltpu.SemaphoreType.DMA((2, len(GROUPS))),
            pltpu.SemaphoreType.DMA((2, len(GROUPS))),
        ],
        compiler_params=pltpu.CompilerParams(
            collective_id=0, has_side_effects=True, vmem_limit_bytes=48 * 2**20
        ),
    )(wavefunction, environments, mpo_terms, sector_dims, channel_charges)
    return psi, energy[0, :1]


def solution(mesh):
    return jax.shard_map(
        body,
        mesh=mesh,
        in_specs=(
            P(("section", "inner"), None, None),
            P(("section", "inner"), None, None),
            P(),
            P(("section", "inner"), None),
            P(),
        ),
        out_specs=(P(("section", "inner"), None, None), P("section")),
        check_vma=False,
    )
```

time: 687 us -> 61.2 us (0.09)
  blocking collectives: 533 us -> 0 us
  Pallas kernels: 0 us -> 56 us
  local copies, waits for them, and re-layouts: 59 us -> 3.18 us
  matrix products: 42.6 us -> 0 us
  other arithmetic: 21.2 us -> 0 us
  between operations: 11.3 us -> 1.83 us
  waiting for transfers between devices: 9.37 us -> 0 us
    psum x7 -> x0, blocking collectives: 533 us -> none  [pair_total(): summed = lax.psum(table, ('section', 'inner'))]
    pallas_call x0 -> x1, Pallas kernels: none -> 56 us  [body(): pl.pallas_call(kernel, out_shape=(jax.ShapeDtypeStruct((1, BLK, WIDTH), F...]
    dot_general x9 -> x0, matrix products: 42.6 us -> none  [the longest x3 17.9 us: apply_operator(): jnp.einsum('kalsr,ast->kaltr', first, mpo_terms, preferred_element_type=j...]
    another operation x5 -> x0, local copies, waits for them, and re-layouts: 38.4 us -> none
    gather x3 -> x0, local copies, waits for them, and re-layouts: 12.8 us -> none  [apply_operator(): sources = jnp.take(stacked, channel_charges + 1, axis=0)]
    reduce_sum x14 -> x0, other arithmetic: 9.55 us -> none  [the longest x7 3.23 us: pair_total(): totals = jnp.sum(selector[:, None] * summed, axis=0)]
    ppermute x7 -> x0, waiting for transfers between devices: 9.37 us -> none  [the longest x3 5.48 us: with_halo(): after = lax.ppermute(first, axis, down)]
  transfers between devices with their start and end apart: 7 -> 0, of which waited for: 4 -> 0; matrix products, arithmetic and copies ran while one was open for 1% -> 0% of each run, Pallas kernels for 0% -> 0%
where the time goes in v1:
time: 61.2 us; the launch traced here: 61.1 us
  Pallas kernels  56 us (92%)
  local copies, waits for them, and re-layouts  3.18 us (5%)
  between operations  1.83 us (3%)
    pallas_call x1, Pallas kernels, body(): pl.pallas_call(kernel, out_shape=(jax.ShapeDtypeStruct((1, BLK, WIDTH), F...  56 us
    unnamed x9, local copies, waits for them, and re-layouts  3.18 us

profile of v1, /device:TPU:1, one launch (start us, length us, event | category | flops | bytes accessed | tf_op | source)
XLA Modules:
  0.0 61.1 jit_solution(13436029221425227898)
XLA Ops:
  0.6 1.1 %copy.8.mpo_ref = bf16[34,16,16]{2,1,0:T(8,128)(2,1)S(1)} copy(bf16[34,16,16]{0,2,1:T(8,128)(2,1)} %param.7) | data formatting | bytes 34816 | tf_op args[2]
  1.7 0.0 copy-start
  1.7 0.0 copy-start.1
  1.7 0.0 copy-start.2
  1.7 1.4 %copy.7.env_ref = bf16[2,34,4096]{2,1,0:T(8,128)(2,1)S(1)} copy(bf16[2,34,4096]{2,0,1:T(2,128)(2,1)} %param.6) | data formatting | bytes 1114112 | tf_op args[1]
  3.1 0.0 copy-done
  3.1 0.0 copy-done.1
  3.1 0.0 copy-done.2
  3.1 56.0 %shard_map.68 = (f32[1,64,1024]{2,1,0:T(8,128)S(1)}, f32[1,128]{1,0:T(1,128)S(1)}) custom-call(f32[1,64,1024]{2,1,0:T(8,128)S(1)} %copy-done, bf16[2,34,4096]{2,1,0:T(8,128)(2,1)S(1)} %copy.7.env_ref, bf16[34,16,16]{2,1,0:T(8,128)(2,1)S(1)} %copy.8.mpo_ref, s32[1,2]{1,0:T(1,128)S(1)} %copy-done.1, s32[34]{0:T(128)S(1)} %copy-done.2), custom_call_target="tpu_custom_call" | custom-call | tf_op jit(solution)/shard_map/pallas_call | solution.py:382
  59.2 0.7 %copy.11 = f32[1,64,1024]{2,1,0:T(8,128)} copy(f32[1,64,1024]{2,1,0:T(8,128)S(1)} %get-tuple-element.8) | data formatting | bytes 524288
Async XLA Ops:
  1.7 1.4 %copy-start = (f32[1,64,1024]{2,1,0:T(8,128)S(1)}, f32[1,64,1024]{2,1,0:T(8,128)}, u32[]{:S(2)}) copy-start(f32[1,64,1024]{2,1,0:T(8,128)} %wave_ref.1) | copy-start | bytes 786436
  1.7 1.4 %copy-start.1 = (s32[1,2]{1,0:T(1,128)S(1)}, s32[1,2]{1,0:T(1,128)}, u32[]{:S(2)}) copy-start(s32[1,2]{1,0:T(1,128)} %dims_ref.1) | copy-start | bytes 28
  1.7 1.4 %copy-start.2 = (s32[34]{0:T(128)S(1)}, s32[34]{0:T(128)}, u32[]{:S(2)}) copy-start(s32[34]{0:T(128)} %charge_ref.1) | copy-start | bytes 412

commit v2 on v1

v2 whole, which is shorter than its diff:
```python
import functools

import jax
import jax.numpy as jnp
from jax import lax
from jax.experimental import pallas as pl
from jax.experimental.pallas import tpu as pltpu
from jax.sharding import PartitionSpec as P

MESH = pl.DeviceIdType.MESH
F32 = jnp.float32
BF16 = jnp.bfloat16

ITERS = 2
EPSILON = 1e-06
BLK = 64
CHAN = 34
PH = 16
WIDTH = PH * BLK
PAIRS = BLK // 2

NEAR = tuple((0, d) for d in range(8))
ACROSS = ((0, 0), (0, 8), (1, 0), (1, 8))
EVERY = tuple((h, d) for h in (0, 1) for d in range(16))

CHUNKS = ((0, 12), (12, 24), (24, CHAN))
GROUP = 6


def flipped(index, bits):
    for bit in (1, 2, 4, 8):
        if bits & bit:
            index = index + bit * (1 - 2 * ((index // bit) % 2))
    return index


def low_half(rows):
    return lax.broadcasted_iota(jnp.int32, (rows, 128), 1) < BLK


def interchange(a, b, low):
    turned_a = pltpu.roll(a, BLK, 1)
    turned_b = pltpu.roll(b, BLK, 1)
    return jnp.where(low, a, turned_b), jnp.where(low, turned_a, b)


def to_mixed(field):
    low = low_half(16)
    rows = []
    for j in range(PH // 2):
        even, odd = [], []
        for p in range(2):
            a = field[32 * p : 32 * p + 16, 128 * j : 128 * j + 128]
            b = field[32 * p + 16 : 32 * p + 32, 128 * j : 128 * j + 128]
            first, second = interchange(a, b, low)
            even.append(first)
            odd.append(second)
        rows.append(jnp.concatenate(even, axis=1))
        rows.append(jnp.concatenate(odd, axis=1))
    return jnp.concatenate(rows, axis=0)


def kernel(
    wave_ref, env_ref, mpo_ref, dims_ref, charge_ref, psi_ref, energy_ref,
    env_buf, wide, raw, outgoing, lsel, rsel, wsel, image, sources,
    halo, mask, columns, start_buf, vec_im, vec_q, vec_t, near_buf, exchange,
    env_load, env_send, env_recv, halo_send, halo_recv, near_send, near_recv, red_send, red_recv,
):
    section, inner = lax.axis_index("section"), lax.axis_index("inner")
    n_inner = lax.axis_size("inner")
    parity = section % 2
    even = parity == 0
    entries = 2.0 * n_inner * BLK * WIDTH

    def at(h, d):
        return (flipped(section, h), flipped(inner, d))

    above = (section, (inner + 1) % n_inner)
    below = (section, (inner + n_inner - 1) % n_inner)
    partner = at(1, 0)

    peers = [partner, above, below] + [at(h, d) for h, d in NEAR[1:] + ACROSS[1:2] + ACROSS[3:]]
    barrier = pltpu.get_barrier_semaphore()
    for peer in peers:
        pl.semaphore_signal(barrier, inc=1, device_id=peer, device_id_type=MESH)

    def env_rows(k, factor):
        first, last = CHUNKS[k]
        return pl.ds(first * PAIRS * factor, (last - first) * PAIRS * factor)

    loads = [
        pltpu.make_async_copy(env_ref.at[env_rows(k, 2)], env_buf.at[env_rows(k, 2)], env_load.at[k])
        for k in range(len(CHUNKS))
    ]
    for load in loads:
        load.start()

    row8 = lax.broadcasted_iota(jnp.int32, (8, 128), 0)
    lane8 = lax.broadcasted_iota(jnp.int32, (8, 128), 1)

    def dots(pairs):
        packed = jnp.zeros((8, 128), F32)
        for k, (x, y) in enumerate(pairs):
            prod = x * y
            tiles = [
                prod[8 * i : 8 * i + 8, 128 * j : 128 * j + 128] for i in range(BLK // 8) for j in range(WIDTH // 128)
            ]
            while len(tiles) > 1:
                tiles = [tiles[2 * n] + tiles[2 * n + 1] for n in range(len(tiles) // 2)]
            tile = tiles[0] + pltpu.roll(tiles[0], 64, 1)
            tile = tile + pltpu.roll(tile, 32, 1)
            packed = jnp.where(lane8 // 32 == k, tile, packed)
        return jnp.sum(packed, axis=0, keepdims=True)

    def send_row(buf, group, value, send, recv):
        buf[0:1, :] = value
        for j, (h, d) in enumerate(group[1:]):
            pltpu.make_async_remote_copy(
                src_ref=buf.at[pl.ds(0, 1)],
                dst_ref=buf.at[pl.ds(j + 1, 1)],
                send_sem=send,
                recv_sem=recv,
                device_id=at(h, d),
                device_id_type=MESH,
            ).start()

    def await_rows(buf, group, sem):
        rows = buf.at[pl.ds(1, len(group) - 1)]
        pltpu.make_async_copy(rows, rows, sem).wait()

    def total_rows(tile):
        for step in (4, 2, 1):
            tile = tile + pltpu.roll(tile, step, 0)
        return tile

    def scalars(tile):
        return jnp.sum(jnp.where(lane8 // 32 == row8, tile, 0.0), axis=1, keepdims=True) * (1.0 / entries)

    def sum_start(k, pairs):
        send_row(exchange.at[k], EVERY, dots(pairs), red_send.at[k], red_recv.at[k])

    def sum_finish(k):
        await_rows(exchange.at[k], EVERY, red_recv.at[k])
        part = [exchange[k, 8 * n : 8 * n + 8, :] for n in range(4)]
        return scalars(total_rows((part[0] + part[1]) + (part[2] + part[3])))

    def halo_copies(k):
        return [
            pltpu.make_async_remote_copy(
                src_ref=halo.at[k, 1],
                dst_ref=halo.at[k, 2 * side],
                send_sem=halo_send.at[k, side],
                recv_sem=halo_recv.at[k, side],
                device_id=target,
                device_id_type=MESH,
            )
            for side, target in ((0, above), (1, below))
        ]

    def channels(first, last):
        groups = [(a, min(a + GROUP, last)) for a in range(first, last, GROUP)]

        def left(group):
            a, b = group
            out = jnp.dot(lsel[a * BLK : b * BLK, :], sources[...], preferred_element_type=F32).astype(BF16)
            return [to_mixed(out[k * BLK : (k + 1) * BLK]) for k in range(b - a)]

        total = None
        ready = left(groups[0])
        for n, (a, b) in enumerate(groups):
            now = ready
            if n + 1 < len(groups):
                ready = left(groups[n + 1])
            mixed = [
                jnp.dot(wsel[a + k], now[k], preferred_element_type=F32).astype(BF16) for k in range(b - a)
            ]
            right = rsel[a:b].reshape((b - a) * 256, 256)
            part = jnp.dot(jnp.concatenate(mixed, axis=1), right, preferred_element_type=F32)
            total = part if total is None else total + part
        return total

    def unmix(total):
        low = low_half(16)
        for j in range(PH // 2):
            for p in range(2):
                a = total[32 * j : 32 * j + 16, 128 * p : 128 * p + 128]
                b = total[32 * j + 16 : 32 * j + 32, 128 * p : 128 * p + 128]
                upper, lower = interchange(a, b, low)
                columns[j, pl.ds(p, 16, stride=2), :] = upper
                columns[j, pl.ds(32 + p, 16, stride=2), :] = lower
        for j in range(PH // 2):
            vec_t[:, 128 * j : 128 * j + 128] = columns[j] * mask[...]

    row = lax.broadcasted_iota(jnp.int32, (BLK, 128), 0)
    lane = lax.broadcasted_iota(jnp.int32, (BLK, 128), 1)
    live = (row < dims_ref[0, 0]) & (lane % BLK < dims_ref[0, 1])
    mask[...] = jnp.where(live, 1.0, 0.0).astype(F32)
    start = wave_ref[0] * jnp.concatenate([mask[...]] * (WIDTH // 128), axis=1)
    start_buf[...] = start
    halo[0, 1] = start.astype(BF16)
    norm_row = dots([(start, start)])

    for k in range(len(CHUNKS)):
        loads[k].wait()
        wide[env_rows(k, 2), :] = env_buf[env_rows(k, 2), :].astype(F32)
        first, last = CHUNKS[k]
        count = (last - first) * PAIRS
        upper = wide[pl.ds(first * PAIRS * 2, count, stride=2), :]
        lower = wide[pl.ds(first * PAIRS * 2 + 1, count, stride=2), :]
        raw[parity, env_rows(k, 1), :] = jnp.where(even, upper, lower).astype(BF16)
        outgoing[env_rows(k, 1), :] = jnp.where(even, lower, upper).astype(BF16)

    pl.semaphore_wait(barrier, len(peers))
    env_copies = [
        pltpu.make_async_remote_copy(
            src_ref=outgoing.at[env_rows(k, 1)],
            dst_ref=raw.at[parity, env_rows(k, 1)],
            send_sem=env_send.at[k],
            recv_sem=env_recv.at[k],
            device_id=partner,
            device_id_type=MESH,
        )
        for k in range(len(CHUNKS))
    ]
    start_halo = halo_copies(0)
    env_copies[0].start()
    for copy in start_halo:
        copy.start()
    for copy in env_copies[1:]:
        copy.start()
    send_row(near_buf.at[0], NEAR, norm_row, near_send.at[0], near_recv.at[0])

    def iota(shape, axis):
        return lax.broadcasted_iota(jnp.int32, shape, axis)

    flat = mpo_ref[...].reshape(PH * PH, CHAN)
    unit_rows = (iota((CHAN, CHAN), 0) == iota((CHAN, CHAN), 1)).astype(BF16)
    by_channel = lax.dot_general(unit_rows, flat, (((1,), (1,)), ((), ())), preferred_element_type=F32)
    keep_t = iota((PH, 256), 1) % 16 == iota((PH, 256), 0)
    picked = jnp.concatenate(
        [jnp.where(keep_t, jnp.broadcast_to(by_channel[a : a + 1, :], (PH, 256)), 0.0) for a in range(CHAN)], axis=0
    ).astype(BF16)
    widen = (iota((256, 256), 0) // 16 == iota((256, 256), 1) // 16).astype(BF16)
    terms = jnp.dot(picked, widen, preferred_element_type=F32).astype(BF16)
    spread_rows = (iota((256, PH), 0) // 16 == iota((256, PH), 1)).astype(BF16)
    same = iota((256, 256), 0) % 16 == iota((256, 256), 1) % 16
    for a in range(CHAN):
        both = jnp.dot(spread_rows, terms[a * PH : (a + 1) * PH], preferred_element_type=F32)
        wsel[a] = jnp.where(same, both, 0.0).astype(BF16)

    low32 = low_half(32)
    low64 = low_half(64)

    def doubled(slot, a):
        x = raw[slot, a * PAIRS : (a + 1) * PAIRS, :]
        turned = pltpu.roll(x, BLK, 1)
        return jnp.where(low32, x, turned), jnp.where(low32, turned, x)

    def place_left(first, last):
        for a in range(first, last):
            charge = charge_ref[a]
            here = jnp.where(low32, -1, 0) == charge
            there = jnp.logical_and(low32, charge == 1)
            for half, value in enumerate(doubled(0, a)):
                rows = slice(a * BLK + half * PAIRS, a * BLK + (half + 1) * PAIRS)
                none = jnp.zeros_like(value)
                lsel[rows, 0:128] = jnp.where(here, value, none)
                lsel[rows, 128:192] = jnp.where(there, value, none)[:, :BLK]

    def place_right(first, last):
        none = jnp.zeros((BLK, 128), BF16)
        zero = jnp.zeros((2 * BLK, 128), BF16)
        for a in range(first, last):
            upper, lower = doubled(1, a)
            wide[pl.ds(a * BLK, PAIRS, stride=2), :] = upper.astype(F32)
            wide[pl.ds(a * BLK + 1, PAIRS, stride=2), :] = lower.astype(F32)
            both = wide[a * BLK : (a + 1) * BLK, :].astype(BF16)
            block = jnp.concatenate([jnp.where(low64, both, none), jnp.where(low64, none, both)], axis=0)
            rsel[a, 0:128, 0:128] = block
            rsel[a, 128:256, 128:256] = block
            rsel[a, 0:128, 128:256] = zero
            rsel[a, 128:256, 0:128] = zero

    @pl.when(even)
    def _():
        place_left(0, CHAN)

    @pl.when(jnp.logical_not(even))
    def _():
        place_right(0, CHAN)

    await_rows(near_buf.at[0], NEAR, near_recv.at[0])
    norm_row = total_rows(near_buf[0])[0:1, :]
    send_row(near_buf.at[1], ACROSS, norm_row, near_send.at[1], near_recv.at[1])

    for copy in start_halo:
        copy.wait_recv()
    for k in range(3):
        sources[k * BLK : (k + 1) * BLK, :] = halo[0, k]
    total = None
    for k, (first, last) in enumerate(CHUNKS):
        arrived = raw.at[1 - parity, env_rows(k, 1)]
        pltpu.make_async_copy(arrived, arrived, env_recv.at[k]).wait()

        @pl.when(even)
        def _():
            place_right(first, last)

        @pl.when(jnp.logical_not(even))
        def _():
            place_left(first, last)

        if k:
            image[...] += channels(first, last)
        else:
            image[...] = channels(first, last)

    await_rows(near_buf.at[1], ACROSS, near_recv.at[1])
    part = [near_buf[1, k : k + 1, :] for k in range(4)]
    norm_row = (part[0] + part[1]) + (part[2] + part[3])
    norm = jnp.sum(jnp.where(lane8[0:1] < 32, norm_row, 0.0), axis=1, keepdims=True) * (1.0 / entries)
    scale = 1.0 / jnp.sqrt(norm + EPSILON)
    unmix(image[...])
    im = vec_t[...] * scale
    vec_im[...] = im
    halo[1, 1] = im.astype(BF16)
    halos = [halo_copies(1), halo_copies(2)]
    for copy in halos[0]:
        copy.start()
    psi = start_buf[...] * scale
    start_buf[...] = psi
    sum_start(0, [(psi, im), (im, im)])
    totals = sum_finish(0)

    def scalar(total, k):
        return total[k : k + 1, :]

    energy_now = scalar(totals, 0)
    unit = jnp.sqrt(scalar(totals, 1) + EPSILON)
    inverse = 1.0 / unit

    vec_q[...] = (vec_im[...] - energy_now * start_buf[...]) * inverse
    for copy in halos[0]:
        copy.wait_recv()
    sources[BLK : 2 * BLK, :] = vec_q[...].astype(BF16)
    for k in (0, 2):
        field = (halo[1, k].astype(F32) - (energy_now * scale) * halo[0, k].astype(F32)) * inverse
        sources[k * BLK : (k + 1) * BLK, :] = field.astype(BF16)
    unmix(channels(0, CHAN))
    halo[2, 1] = vec_t[...].astype(BF16)
    for copy in halos[1]:
        copy.start()
    q, t, psi, im = vec_q[...], vec_t[...], start_buf[...], vec_im[...]
    sum_start(1, [(q, q), (q, im), (q, t), (psi, t)])
    totals = sum_finish(1)

    def rotation(energy, coupling, curvature):
        x = 0.5 * (curvature - energy)
        size = jnp.maximum(jnp.abs(x), jnp.abs(coupling))
        safe = jnp.where(size > 0.0, size, 1.0)
        xs, ys = x / safe, -coupling / safe
        radius = jnp.sqrt(xs * xs + ys * ys)
        radius = jnp.where(size > 0.0, radius, 1.0)
        cos2 = jnp.where(size > 0.0, xs / radius, 1.0)
        sin2 = ys / radius
        big = jnp.sqrt(0.5 + 0.5 * jnp.abs(cos2))
        small = 0.5 * sin2 / big
        sign = jnp.where(coupling < 0.0, 1.0, -1.0)
        cosine = jnp.where(cos2 >= 0.0, big, jnp.abs(small))
        sine = jnp.where(cos2 >= 0.0, small, sign * big)
        lowest = 0.5 * (energy + curvature) - jnp.sqrt(x * x + coupling * coupling)
        return cosine, sine, lowest

    def kappa_of(square):
        return unit / jnp.sqrt(unit * unit * square + EPSILON)

    kappa = kappa_of(scalar(totals, 0))
    coupling = kappa * scalar(totals, 1)
    curvature = kappa * kappa * scalar(totals, 2)
    mirrored = kappa * scalar(totals, 3)
    cosine, sine, _ = rotation(energy_now, coupling, curvature)
    energy_next = (
        cosine * cosine * energy_now + cosine * sine * (coupling + mirrored) + sine * sine * curvature
    )
    turn = sine * kappa
    psi = cosine * start_buf[...] + turn * vec_q[...]
    im = cosine * vec_im[...] + turn * vec_t[...]
    start_buf[...] = psi
    vec_im[...] = im
    q = (im - energy_next * psi) * inverse
    vec_q[...] = q
    sources[BLK : 2 * BLK, :] = q.astype(BF16)

    for copy in halos[1]:
        copy.wait_recv()
    for k in (0, 2):
        h_psi = halo[0, k].astype(F32) * scale
        h_im = halo[1, k].astype(F32)
        h_q = (h_im - energy_now * h_psi) * inverse
        n_psi = cosine * h_psi + turn * h_q
        n_im = cosine * h_im + turn * halo[2, k].astype(F32)
        sources[k * BLK : (k + 1) * BLK, :] = ((n_im - energy_next * n_psi) * inverse).astype(BF16)
    unmix(channels(0, CHAN))
    q, t, im = vec_q[...], vec_t[...], vec_im[...]
    sum_start(2, [(q, q), (q, im), (q, t)])
    totals = sum_finish(2)
    kappa = kappa_of(scalar(totals, 0))
    coupling = kappa * scalar(totals, 1)
    curvature = kappa * kappa * scalar(totals, 2)
    cosine, sine, lowest = rotation(energy_next, coupling, curvature)
    psi_ref[0] = cosine * start_buf[...] + (sine * kappa) * vec_q[...]
    energy_ref[...] = jnp.broadcast_to(lowest, (1, 128))

    await_rows(near_buf.at[0], NEAR, near_send.at[0])
    await_rows(near_buf.at[1], ACROSS, near_send.at[1])
    for k in range(3):
        await_rows(exchange.at[k], EVERY, red_send.at[k])
    for copies in [env_copies, start_halo] + halos:
        for copy in copies:
            copy.wait_send()


def body(wavefunction, environments, mpo_terms, sector_dims, channel_charges):
    rows = environments.reshape(2, CHAN, PAIRS, 128).transpose(1, 2, 0, 3).reshape(CHAN * PAIRS * 2, 128)
    terms = mpo_terms.transpose(1, 2, 0)
    vmem = pl.BlockSpec(memory_space=pltpu.VMEM)
    smem = pl.BlockSpec(memory_space=pltpu.SMEM)
    psi, energy = pl.pallas_call(
        kernel,
        out_shape=(
            jax.ShapeDtypeStruct((1, BLK, WIDTH), F32),
            jax.ShapeDtypeStruct((1, 128), F32),
        ),
        in_specs=[vmem, pl.BlockSpec(memory_space=pl.ANY), vmem, smem, smem],
        out_specs=(vmem, vmem),
        scratch_shapes=[
            pltpu.VMEM((2 * CHAN * PAIRS, 128), BF16),
            pltpu.VMEM((2 * CHAN * PAIRS, 128), F32),
            pltpu.VMEM((2, CHAN * PAIRS, 128), BF16),
            pltpu.VMEM((CHAN * PAIRS, 128), BF16),
            pltpu.VMEM((CHAN * BLK, 3 * BLK), BF16),
            pltpu.VMEM((CHAN, 256, 256), BF16),
            pltpu.VMEM((CHAN, 256, 256), BF16),
            pltpu.VMEM((256, 256), F32),
            pltpu.VMEM((3 * BLK, WIDTH), BF16),
            pltpu.VMEM((3, 3, BLK, WIDTH), BF16),
            pltpu.VMEM((BLK, 128), F32),
            pltpu.VMEM((PH // 2, BLK, 128), F32),
            pltpu.VMEM((BLK, WIDTH), F32),
            pltpu.VMEM((BLK, WIDTH), F32),
            pltpu.VMEM((BLK, WIDTH), F32),
            pltpu.VMEM((BLK, WIDTH), F32),
            pltpu.VMEM((2, 8, 128), F32),
            pltpu.VMEM((3, 32, 128), F32),
            pltpu.SemaphoreType.DMA((len(CHUNKS),)),
            pltpu.SemaphoreType.DMA((len(CHUNKS),)),
            pltpu.SemaphoreType.DMA((len(CHUNKS),)),
            pltpu.SemaphoreType.DMA((3, 2)),
            pltpu.SemaphoreType.DMA((3, 2)),
            pltpu.SemaphoreType.DMA((2,)),
            pltpu.SemaphoreType.DMA((2,)),
            pltpu.SemaphoreType.DMA((3,)),
            pltpu.SemaphoreType.DMA((3,)),
        ],
        compiler_params=pltpu.CompilerParams(
            collective_id=0, has_side_effects=True, vmem_limit_bytes=60 * 2**20
        ),
    )(wavefunction, rows, terms, sector_dims, channel_charges)
    return psi, energy[0, :1]


def solution(mesh):
    return jax.shard_map(
        body,
        mesh=mesh,
        in_specs=(
            P(("section", "inner"), None, None),
            P(("section", "inner"), None, None),
            P(),
            P(("section", "inner"), None),
            P(),
        ),
        out_specs=(P(("section", "inner"), None, None), P("section")),
        check_vma=False,
    )
```

time: 61.2 us -> 46.3 us (0.76)
  Pallas kernels: 56 us -> 42.6 us
  local copies, waits for them, and re-layouts: 3.18 us -> 1.68 us
    pallas_call x1, Pallas kernels: 56 us -> 42.6 us  [body(): pl.pallas_call(kernel, out_shape=(jax.ShapeDtypeStruct((1, BLK, WIDTH), F...]
    unnamed x9 -> x3, local copies, waits for them, and re-layouts: 3.18 us -> 1.68 us
where the time goes in v2:
time: 46.3 us; the launch traced here: 46.1 us
  Pallas kernels  42.6 us (92%)
  between operations  1.81 us (4%)
  local copies, waits for them, and re-layouts  1.68 us (4%)
    pallas_call x1, Pallas kernels, body(): pl.pallas_call(kernel, out_shape=(jax.ShapeDtypeStruct((1, BLK, WIDTH), F...  42.6 us
    unnamed x3, local copies, waits for them, and re-layouts  1.68 us

profile of v2, /device:TPU:1, one launch (start us, length us, event | category | flops | bytes accessed | tf_op | source)
XLA Modules:
  0.0 46.1 jit_solution(12525736599203480689)
XLA Ops:
  0.6 42.6 %shard_map.68 = (f32[1,64,1024]{2,1,0:T(8,128)}, f32[1,128]{1,0:T(1,128)}) custom-call(f32[1,64,1024]{2,1,0:T(8,128)} %wave_ref.1, bf16[2176,128]{1,0:T(8,128)(2,1)} %bitcast.8, bf16[16,16,34]{2,1,0:T(8,128)(2,1)} %bitcast.9, s32[1,2]{1,0:T(1,128)} %dims_ref.1, s32[34]{0:T(128)} %charge_ref.1), custom_call_target="tpu_custom_call" | custom-call | tf_op jit(solution)/shard_map/pallas_call | solution.py:428
  43.3 0.0 copy-start
  43.3 1.7 %copy.10 = f32[1,64,1024]{2,1,0:T(8,128)} copy(f32[1,64,1024]{2,1,0:T(8,128)} %get-tuple-element.8) | data formatting | bytes 524288
  44.9 0.0 copy-done
Async XLA Ops:
  43.3 1.7 %copy-start = (f32[1,128]{1,0:T(1,128)S(1)}, f32[1,128]{1,0:T(1,128)}, u32[]{:S(2)}) copy-start(f32[1,128]{1,0:T(1,128)} %get-tuple-element.5) | copy-start | bytes 1540

commit v3 on v2

--- a/solution.py
+++ b/solution.py
@@ -23,8 +23,14 @@
 ACROSS = ((0, 0), (0, 8), (1, 0), (1, 8))
 EVERY = tuple((h, d) for h in (0, 1) for d in range(16))
 
+
+def distance(peer):
+    h, d = peer
+    return h + (d & 8) // 8 + (2 if d & 6 == 4 else 1 if d & 6 else 0)
+
+
 CHUNKS = ((0, 12), (12, 24), (24, CHAN))
-GROUP = 6
+GROUP = 4
 
 
 def flipped(index, bits):
@@ -61,10 +67,10 @@
 
 
 def kernel(
-    wave_ref, env_ref, mpo_ref, dims_ref, charge_ref, psi_ref, energy_ref,
-    env_buf, wide, raw, outgoing, lsel, rsel, wsel, image, sources,
+    wave_hbm, env_ref, mpo_hbm, dims_hbm, charge_hbm, psi_ref, energy_ref,
+    wave_ref, mpo_ref, dims_ref, charge_ref, env_buf, wide, raw, outgoing, lsel, rsel, wsel, image, sources,
     halo, mask, columns, start_buf, vec_im, vec_q, vec_t, near_buf, exchange,
-    env_load, env_send, env_recv, halo_send, halo_recv, near_send, near_recv, red_send, red_recv,
+    small_load, env_load, env_send, env_recv, halo_send, halo_recv, near_send, near_recv, red_send, red_recv,
 ):
     section, inner = lax.axis_index("section"), lax.axis_index("inner")
     n_inner = lax.axis_size("inner")
@@ -84,6 +90,15 @@
     for peer in peers:
         pl.semaphore_signal(barrier, inc=1, device_id=peer, device_id_type=MESH)
 
+    small = [
+        pltpu.make_async_copy(source, target, small_load.at[k])
+        for k, (source, target) in enumerate(
+            ((dims_hbm, dims_ref), (wave_hbm, wave_ref), (mpo_hbm, mpo_ref), (charge_hbm, charge_ref))
+        )
+    ]
+    small[0].start()
+    small[1].start()
+
     def env_rows(k, factor):
         first, last = CHUNKS[k]
         return pl.ds(first * PAIRS * factor, (last - first) * PAIRS * factor)
@@ -92,7 +107,7 @@
         pltpu.make_async_copy(env_ref.at[env_rows(k, 2)], env_buf.at[env_rows(k, 2)], env_load.at[k])
         for k in range(len(CHUNKS))
     ]
-    for load in loads:
+    for load in loads + small[2:]:
         load.start()
 
     row8 = lax.broadcasted_iota(jnp.int32, (8, 128), 0)
@@ -114,10 +129,11 @@
 
     def send_row(buf, group, value, send, recv):
         buf[0:1, :] = value
-        for j, (h, d) in enumerate(group[1:]):
+        for h, d in sorted(group[1:], key=distance, reverse=True):
+            j = group.index((h, d))
             pltpu.make_async_remote_copy(
                 src_ref=buf.at[pl.ds(0, 1)],
-                dst_ref=buf.at[pl.ds(j + 1, 1)],
+                dst_ref=buf.at[pl.ds(j, 1)],
                 send_sem=send,
                 recv_sem=recv,
                 device_id=at(h, d),
@@ -191,6 +207,8 @@
         for j in range(PH // 2):
             vec_t[:, 128 * j : 128 * j + 128] = columns[j] * mask[...]
 
+    small[0].wait()
+    small[1].wait()
     row = lax.broadcasted_iota(jnp.int32, (BLK, 128), 0)
     lane = lax.broadcasted_iota(jnp.int32, (BLK, 128), 1)
     live = (row < dims_ref[0, 0]) & (lane % BLK < dims_ref[0, 1])
@@ -233,6 +251,8 @@
     def iota(shape, axis):
         return lax.broadcasted_iota(jnp.int32, shape, axis)
 
+    small[2].wait()
+    small[3].wait()
     flat = mpo_ref[...].reshape(PH * PH, CHAN)
     unit_rows = (iota((CHAN, CHAN), 0) == iota((CHAN, CHAN), 1)).astype(BF16)
     by_channel = lax.dot_general(unit_rows, flat, (((1,), (1,)), ((), ())), preferred_element_type=F32)
@@ -424,16 +444,20 @@
     rows = environments.reshape(2, CHAN, PAIRS, 128).transpose(1, 2, 0, 3).reshape(CHAN * PAIRS * 2, 128)
     terms = mpo_terms.transpose(1, 2, 0)
     vmem = pl.BlockSpec(memory_space=pltpu.VMEM)
-    smem = pl.BlockSpec(memory_space=pltpu.SMEM)
+    hbm = pl.BlockSpec(memory_space=pltpu.HBM)
     psi, energy = pl.pallas_call(
         kernel,
         out_shape=(
-            jax.ShapeDtypeStruct((1, BLK, WIDTH), F32),
-            jax.ShapeDtypeStruct((1, 128), F32),
+            pltpu.VMEM((1, BLK, WIDTH), F32),
+            pltpu.VMEM((1, 128), F32),
         ),
-        in_specs=[vmem, pl.BlockSpec(memory_space=pl.ANY), vmem, smem, smem],
+        in_specs=[hbm] * 5,
         out_specs=(vmem, vmem),
         scratch_shapes=[
+            pltpu.VMEM((1, BLK, WIDTH), F32),
+            pltpu.VMEM((PH, PH, CHAN), BF16),
+            pltpu.SMEM((1, 2), jnp.int32),
+            pltpu.SMEM((CHAN,), jnp.int32),
             pltpu.VMEM((2 * CHAN * PAIRS, 128), BF16),
             pltpu.VMEM((2 * CHAN * PAIRS, 128), F32),
             pltpu.VMEM((2, CHAN * PAIRS, 128), BF16),
@@ -452,6 +476,7 @@
             pltpu.VMEM((BLK, WIDTH), F32),
             pltpu.VMEM((2, 8, 128), F32),
             pltpu.VMEM((3, 32, 128), F32),
+            pltpu.SemaphoreType.DMA((4,)),
             pltpu.SemaphoreType.DMA((len(CHUNKS),)),
             pltpu.SemaphoreType.DMA((len(CHUNKS),)),
             pltpu.SemaphoreType.DMA((len(CHUNKS),)),
@@ -463,7 +488,7 @@
             pltpu.SemaphoreType.DMA((3,)),
         ],
         compiler_params=pltpu.CompilerParams(
-            collective_id=0, has_side_effects=True, vmem_limit_bytes=60 * 2**20
+            collective_id=0, has_side_effects=True, vmem_limit_bytes=56 * 2**20
         ),
     )(wavefunction, rows, terms, sector_dims, channel_charges)
     return psi, energy[0, :1]

time: 46.3 us -> 42.8 us (0.924)
  Pallas kernels: 42.6 us -> 40.1 us
  local copies, waits for them, and re-layouts: 1.68 us -> 0.71 us
    pallas_call x1, Pallas kernels: 42.6 us -> 40.1 us  [body(): pl.pallas_call(kernel, out_shape=(pltpu.VMEM((1, BLK, WIDTH), F32), pltpu...]
    unnamed x3 -> x1, local copies, waits for them, and re-layouts: 1.68 us -> 0.71 us
where the time goes in v3:
time: 42.8 us; the launch traced here: 42.6 us
  Pallas kernels  40.1 us (94%)
  between operations  1.8 us (4%)
  local copies, waits for them, and re-layouts  0.71 us (2%)
    pallas_call x1, Pallas kernels, body(): pl.pallas_call(kernel, out_shape=(pltpu.VMEM((1, BLK, WIDTH), F32), pltpu...  40.1 us

profile of v3, /device:TPU:1, one launch (start us, length us, event | category | flops | bytes accessed | tf_op | source)
XLA Modules:
  0.0 42.6 jit_solution(4724663589477574172)
XLA Ops:
  0.6 40.1 %shard_map.68 = (f32[1,64,1024]{2,1,0:T(8,128)S(1)}, f32[1,128]{1,0:T(1,128)S(1)}) custom-call(f32[1,64,1024]{2,1,0:T(8,128)} %wave_hbm.1, bf16[2176,128]{1,0:T(8,128)(2,1)} %bitcast.9, bf16[16,16,34]{2,1,0:T(8,128)(2,1)} %bitcast.10, s32[1,2]{1,0:T(1,128)} %dims_hbm.1, s32[34]{0:T(128)} %charge_hbm.1), custom_call_target="tpu_custom_call" | custom-call | tf_op jit(solution)/shard_map/pallas_call | solution.py:448
  40.8 0.7 %copy.10 = f32[1,64,1024]{2,1,0:T(8,128)} copy(f32[1,64,1024]{2,1,0:T(8,128)S(1)} %get-tuple-element.6) | data formatting | bytes 524288

commit v4 on v3

--- a/solution.py
+++ b/solution.py
@@ -69,7 +69,7 @@
 def kernel(
     wave_hbm, env_ref, mpo_hbm, dims_hbm, charge_hbm, psi_ref, energy_ref,
     wave_ref, mpo_ref, dims_ref, charge_ref, env_buf, wide, raw, outgoing, lsel, rsel, wsel, image, sources,
-    halo, mask, columns, start_buf, vec_im, vec_q, vec_t, near_buf, exchange,
+    halo, mask, columns, start_buf, im_buf, vec_im, vec_q, vec_t, near_buf, exchange,
     small_load, env_load, env_send, env_recv, halo_send, halo_recv, near_send, near_recv, red_send, red_recv,
 ):
     section, inner = lax.axis_index("section"), lax.axis_index("inner")
@@ -152,8 +152,8 @@
     def scalars(tile):
         return jnp.sum(jnp.where(lane8 // 32 == row8, tile, 0.0), axis=1, keepdims=True) * (1.0 / entries)
 
-    def sum_start(k, pairs):
-        send_row(exchange.at[k], EVERY, dots(pairs), red_send.at[k], red_recv.at[k])
+    def sum_start(k, row):
+        send_row(exchange.at[k], EVERY, row, red_send.at[k], red_recv.at[k])
 
     def sum_finish(k):
         await_rows(exchange.at[k], EVERY, red_recv.at[k])
@@ -173,7 +173,7 @@
             for side, target in ((0, above), (1, below))
         ]
 
-    def channels(first, last):
+    def channels(first, last, midway=None):
         groups = [(a, min(a + GROUP, last)) for a in range(first, last, GROUP)]
 
         def left(group):
@@ -187,6 +187,8 @@
             now = ready
             if n + 1 < len(groups):
                 ready = left(groups[n + 1])
+            if midway is not None and n == len(groups) // 2:
+                midway()
             mixed = [
                 jnp.dot(wsel[a + k], now[k], preferred_element_type=F32).astype(BF16) for k in range(b - a)
             ]
@@ -349,30 +351,9 @@
         copy.start()
     psi = start_buf[...] * scale
     start_buf[...] = psi
-    sum_start(0, [(psi, im), (im, im)])
-    totals = sum_finish(0)
 
     def scalar(total, k):
         return total[k : k + 1, :]
-
-    energy_now = scalar(totals, 0)
-    unit = jnp.sqrt(scalar(totals, 1) + EPSILON)
-    inverse = 1.0 / unit
-
-    vec_q[...] = (vec_im[...] - energy_now * start_buf[...]) * inverse
-    for copy in halos[0]:
-        copy.wait_recv()
-    sources[BLK : 2 * BLK, :] = vec_q[...].astype(BF16)
-    for k in (0, 2):
-        field = (halo[1, k].astype(F32) - (energy_now * scale) * halo[0, k].astype(F32)) * inverse
-        sources[k * BLK : (k + 1) * BLK, :] = field.astype(BF16)
-    unmix(channels(0, CHAN))
-    halo[2, 1] = vec_t[...].astype(BF16)
-    for copy in halos[1]:
-        copy.start()
-    q, t, psi, im = vec_q[...], vec_t[...], start_buf[...], vec_im[...]
-    sum_start(1, [(q, q), (q, im), (q, t), (psi, t)])
-    totals = sum_finish(1)
 
     def rotation(energy, coupling, curvature):
         x = 0.5 * (curvature - energy)
@@ -394,6 +375,61 @@
     def kappa_of(square):
         return unit / jnp.sqrt(unit * unit * square + EPSILON)
 
+    def own(row):
+        return scalars(jnp.broadcast_to(row, (8, 128)))
+
+    share = 1.0 / (2 * n_inner)
+    row_sums = dots([(psi, im), (im, im), (psi, psi)])
+    sum_start(0, row_sums)
+    local = own(row_sums)
+    weight = jnp.maximum(scalar(local, 2), 0.5 * share)
+    quotient = scalar(local, 0) / weight
+    sources[BLK : 2 * BLK, :] = (vec_im[...] - quotient * start_buf[...]).astype(BF16)
+    scaled = quotient * scale
+    for copy in halos[0]:
+        copy.wait_recv()
+    for k in (0, 2):
+        field = halo[1, k].astype(F32) - scaled * halo[0, k].astype(F32)
+        sources[k * BLK : (k + 1) * BLK, :] = field.astype(BF16)
+    sums = {}
+
+    def read_first():
+        sums[0] = sum_finish(0)
+
+    unmix(channels(0, CHAN, read_first))
+    energy_now = scalar(sums[0], 0)
+    square = scalar(sums[0], 1)
+    unit = jnp.sqrt(square + EPSILON)
+    inverse = 1.0 / unit
+    t = (vec_t[...] + (quotient - energy_now) * vec_im[...]) * inverse
+    vec_t[...] = t
+    halo[2, 1] = t.astype(BF16)
+    for copy in halos[1]:
+        copy.start()
+    q = (vec_im[...] - energy_now * start_buf[...]) * inverse
+    vec_q[...] = q
+
+    row_sums = dots([(q, q), (q, vec_im[...]), (q, vec_t[...]), (start_buf[...], vec_t[...])])
+    sum_start(1, row_sums)
+    local = own(row_sums)
+    rest = square + energy_now * (energy_now * scalar(sums[0], 2) - 2.0 * energy_now)
+    floor = 0.5 * share * jnp.maximum(rest * inverse * inverse, 1e-6)
+    along_q = scalar(local, 2) / jnp.maximum(scalar(local, 0), floor)
+    along_psi = scalar(local, 3) / weight
+    sources[BLK : 2 * BLK, :] = (vec_t[...] - along_q * vec_q[...] - along_psi * start_buf[...]).astype(BF16)
+    of_im = along_q * inverse
+    of_start = (along_psi - of_im * energy_now) * scale
+    for copy in halos[1]:
+        copy.wait_recv()
+    for k in (0, 2):
+        field = halo[2, k].astype(F32) - of_im * halo[1, k].astype(F32) - of_start * halo[0, k].astype(F32)
+        sources[k * BLK : (k + 1) * BLK, :] = field.astype(BF16)
+
+    def read_second():
+        sums[1] = sum_finish(1)
+
+    turned_t = channels(0, CHAN, read_second)
+    totals = sums[1]
     kappa = kappa_of(scalar(totals, 0))
     coupling = kappa * scalar(totals, 1)
     curvature = kappa * kappa * scalar(totals, 2)
@@ -405,24 +441,15 @@
     turn = sine * kappa
     psi = cosine * start_buf[...] + turn * vec_q[...]
     im = cosine * vec_im[...] + turn * vec_t[...]
+    known = (cosine * unit + turn * along_q) * vec_t[...] + (cosine * energy_now + turn * along_psi) * vec_im[...]
     start_buf[...] = psi
-    vec_im[...] = im
     q = (im - energy_next * psi) * inverse
     vec_q[...] = q
-    sources[BLK : 2 * BLK, :] = q.astype(BF16)
-
-    for copy in halos[1]:
-        copy.wait_recv()
-    for k in (0, 2):
-        h_psi = halo[0, k].astype(F32) * scale
-        h_im = halo[1, k].astype(F32)
-        h_q = (h_im - energy_now * h_psi) * inverse
-        n_psi = cosine * h_psi + turn * h_q
-        n_im = cosine * h_im + turn * halo[2, k].astype(F32)
-        sources[k * BLK : (k + 1) * BLK, :] = ((n_im - energy_next * n_psi) * inverse).astype(BF16)
-    unmix(channels(0, CHAN))
-    q, t, im = vec_q[...], vec_t[...], vec_im[...]
-    sum_start(2, [(q, q), (q, im), (q, t)])
+    vec_im[...] = known - energy_next * im
+    im_buf[...] = im
+    unmix(turned_t)
+    t = (vec_im[...] + turn * vec_t[...]) * inverse
+    sum_start(2, dots([(vec_q[...], vec_q[...]), (vec_q[...], im_buf[...]), (vec_q[...], t)]))
     totals = sum_finish(2)
     kappa = kappa_of(scalar(totals, 0))
     coupling = kappa * scalar(totals, 1)
@@ -474,6 +501,7 @@
             pltpu.VMEM((BLK, WIDTH), F32),
             pltpu.VMEM((BLK, WIDTH), F32),
             pltpu.VMEM((BLK, WIDTH), F32),
+            pltpu.VMEM((BLK, WIDTH), F32),
             pltpu.VMEM((2, 8, 128), F32),
             pltpu.VMEM((3, 32, 128), F32),
             pltpu.SemaphoreType.DMA((4,)),

time: 42.8 us -> 41.4 us (0.967)
  Pallas kernels: 40.1 us -> 38.8 us
    pallas_call x1, Pallas kernels: 40.1 us -> 38.8 us  [body(): pl.pallas_call(kernel, out_shape=(pltpu.VMEM((1, BLK, WIDTH), F32), pltpu...]
where the time goes in v4:
time: 41.4 us; the launch traced here: 41.3 us
  Pallas kernels  38.8 us (94%)
  between operations  1.8 us (4%)
  local copies, waits for them, and re-layouts  0.71 us (2%)
    pallas_call x1, Pallas kernels, body(): pl.pallas_call(kernel, out_shape=(pltpu.VMEM((1, BLK, WIDTH), F32), pltpu...  38.8 us

profile of v4, /device:TPU:1, one launch (start us, length us, event | category | flops | bytes accessed | tf_op | source)
XLA Modules:
  0.0 41.3 jit_solution(14893577469327287837)
XLA Ops:
  0.6 38.8 %shard_map.68 = (f32[1,64,1024]{2,1,0:T(8,128)S(1)}, f32[1,128]{1,0:T(1,128)S(1)}) custom-call(f32[1,64,1024]{2,1,0:T(8,128)} %wave_hbm.1, bf16[2176,128]{1,0:T(8,128)(2,1)} %bitcast.9, bf16[16,16,34]{2,1,0:T(8,128)(2,1)} %bitcast.10, s32[1,2]{1,0:T(1,128)} %dims_hbm.1, s32[34]{0:T(128)} %charge_hbm.1), custom_call_target="tpu_custom_call" | custom-call | tf_op jit(solution)/shard_map/pallas_call | solution.py:475
  39.4 0.7 %copy.10 = f32[1,64,1024]{2,1,0:T(8,128)} copy(f32[1,64,1024]{2,1,0:T(8,128)S(1)} %get-tuple-element.6) | data formatting | bytes 524288

commit v5 on v4

--- a/solution.py
+++ b/solution.py
@@ -29,7 +29,7 @@
     return h + (d & 8) // 8 + (2 if d & 6 == 4 else 1 if d & 6 else 0)
 
 
-CHUNKS = ((0, 12), (12, 24), (24, CHAN))
+CHUNKS = ((0, 18), (18, CHAN))
 GROUP = 4
 
 
@@ -68,8 +68,8 @@
 
 def kernel(
     wave_hbm, env_ref, mpo_hbm, dims_hbm, charge_hbm, psi_ref, energy_ref,
-    wave_ref, mpo_ref, dims_ref, charge_ref, env_buf, wide, raw, outgoing, lsel, rsel, wsel, image, sources,
-    halo, mask, columns, start_buf, im_buf, vec_im, vec_q, vec_t, near_buf, exchange,
+    wave_ref, mpo_ref, dims_ref, charge_ref, env_buf, wide, woven, raw, outgoing, lsel, rsel, wsel, image, sources,
+    halo, mask, start_buf, im_buf, vec_im, vec_q, vec_t, near_buf, exchange,
     small_load, env_load, env_send, env_recv, halo_send, halo_recv, near_send, near_recv, red_send, red_recv,
 ):
     section, inner = lax.axis_index("section"), lax.axis_index("inner")
@@ -78,8 +78,11 @@
     even = parity == 0
     entries = 2.0 * n_inner * BLK * WIDTH
 
+    sections = [flipped(section, h) for h in (0, 1)]
+    inners = [flipped(inner, d) for d in range(16)]
+
     def at(h, d):
-        return (flipped(section, h), flipped(inner, d))
+        return (sections[h], inners[d])
 
     above = (section, (inner + 1) % n_inner)
     below = (section, (inner + n_inner - 1) % n_inner)
@@ -113,19 +116,24 @@
     row8 = lax.broadcasted_iota(jnp.int32, (8, 128), 0)
     lane8 = lax.broadcasted_iota(jnp.int32, (8, 128), 1)
 
+    def partial(x, y):
+        prod = x * y
+        tiles = [
+            prod[8 * i : 8 * i + 8, 128 * j : 128 * j + 128] for i in range(BLK // 8) for j in range(WIDTH // 128)
+        ]
+        while len(tiles) > 1:
+            tiles = [tiles[2 * n] + tiles[2 * n + 1] for n in range(len(tiles) // 2)]
+        tile = tiles[0] + pltpu.roll(tiles[0], 64, 1)
+        return tile + pltpu.roll(tile, 32, 1)
+
+    def packed(tiles):
+        total = jnp.zeros((8, 128), F32)
+        for k, tile in enumerate(tiles):
+            total = jnp.where(lane8 // 32 == k, tile, total)
+        return jnp.sum(total, axis=0, keepdims=True)
+
     def dots(pairs):
-        packed = jnp.zeros((8, 128), F32)
-        for k, (x, y) in enumerate(pairs):
-            prod = x * y
-            tiles = [
-                prod[8 * i : 8 * i + 8, 128 * j : 128 * j + 128] for i in range(BLK // 8) for j in range(WIDTH // 128)
-            ]
-            while len(tiles) > 1:
-                tiles = [tiles[2 * n] + tiles[2 * n + 1] for n in range(len(tiles) // 2)]
-            tile = tiles[0] + pltpu.roll(tiles[0], 64, 1)
-            tile = tile + pltpu.roll(tile, 32, 1)
-            packed = jnp.where(lane8 // 32 == k, tile, packed)
-        return jnp.sum(packed, axis=0, keepdims=True)
+        return packed([partial(x, y) for x, y in pairs])
 
     def send_row(buf, group, value, send, recv):
         buf[0:1, :] = value
@@ -173,8 +181,8 @@
             for side, target in ((0, above), (1, below))
         ]
 
-    def channels(first, last, midway=None):
-        groups = [(a, min(a + GROUP, last)) for a in range(first, last, GROUP)]
+    def channels(first, last, midway=None, size=GROUP):
+        groups = [(a, min(a + size, last)) for a in range(first, last, size)]
 
         def left(group):
             a, b = group
@@ -200,14 +208,13 @@
     def unmix(total):
         low = low_half(16)
         for j in range(PH // 2):
+            lanes = slice(128 * j, 128 * j + 128)
             for p in range(2):
                 a = total[32 * j : 32 * j + 16, 128 * p : 128 * p + 128]
                 b = total[32 * j + 16 : 32 * j + 32, 128 * p : 128 * p + 128]
-                upper, lower = interchange(a, b, low)
-                columns[j, pl.ds(p, 16, stride=2), :] = upper
-                columns[j, pl.ds(32 + p, 16, stride=2), :] = lower
-        for j in range(PH // 2):
-            vec_t[:, 128 * j : 128 * j + 128] = columns[j] * mask[...]
+                for half, value in enumerate(interchange(a, b, low)):
+                    rows = slice(32 * p + 16 * half, 32 * p + 16 * half + 16)
+                    vec_t[rows, lanes] = value * mask[rows, :]
 
     small[0].wait()
     small[1].wait()
@@ -227,8 +234,15 @@
         count = (last - first) * PAIRS
         upper = wide[pl.ds(first * PAIRS * 2, count, stride=2), :]
         lower = wide[pl.ds(first * PAIRS * 2 + 1, count, stride=2), :]
-        raw[parity, env_rows(k, 1), :] = jnp.where(even, upper, lower).astype(BF16)
-        outgoing[env_rows(k, 1), :] = jnp.where(even, lower, upper).astype(BF16)
+        for side, value in enumerate((jnp.where(even, upper, lower), jnp.where(even, lower, upper))):
+            for a in range(last - first):
+                here = (first + a) * PAIRS
+                x, y = value[a * PAIRS : a * PAIRS + 16], value[a * PAIRS + 16 : (a + 1) * PAIRS]
+                evens, odds = interchange(x, y, low_half(16))
+                woven[side, pl.ds(here, 16, stride=2), :] = evens
+                woven[side, pl.ds(here + 1, 16, stride=2), :] = odds
+        raw[parity, env_rows(k, 1), :] = woven[0, env_rows(k, 1), :].astype(BF16)
+        outgoing[env_rows(k, 1), :] = woven[1, env_rows(k, 1), :].astype(BF16)
 
     pl.semaphore_wait(barrier, len(peers))
     env_copies = [
@@ -250,6 +264,11 @@
         copy.start()
     send_row(near_buf.at[0], NEAR, norm_row, near_send.at[0], near_recv.at[0])
 
+    zero = jnp.zeros((2 * BLK, 128), BF16)
+    for a in range(CHAN):
+        rsel[a, 0:128, 128:256] = zero
+        rsel[a, 128:256, 0:128] = zero
+
     def iota(shape, axis):
         return lax.broadcasted_iota(jnp.int32, shape, axis)
 
@@ -291,17 +310,11 @@
 
     def place_right(first, last):
         none = jnp.zeros((BLK, 128), BF16)
-        zero = jnp.zeros((2 * BLK, 128), BF16)
         for a in range(first, last):
-            upper, lower = doubled(1, a)
-            wide[pl.ds(a * BLK, PAIRS, stride=2), :] = upper.astype(F32)
-            wide[pl.ds(a * BLK + 1, PAIRS, stride=2), :] = lower.astype(F32)
-            both = wide[a * BLK : (a + 1) * BLK, :].astype(BF16)
+            both = jnp.concatenate(doubled(1, a), axis=0)
             block = jnp.concatenate([jnp.where(low64, both, none), jnp.where(low64, none, both)], axis=0)
             rsel[a, 0:128, 0:128] = block
             rsel[a, 128:256, 128:256] = block
-            rsel[a, 0:128, 128:256] = zero
-            rsel[a, 128:256, 0:128] = zero
 
     @pl.when(even)
     def _():
@@ -315,23 +328,27 @@
     norm_row = total_rows(near_buf[0])[0:1, :]
     send_row(near_buf.at[1], ACROSS, norm_row, near_send.at[1], near_recv.at[1])
 
+    def receive(k):
+        first, last = CHUNKS[k]
+        arrived = raw.at[1 - parity, env_rows(k, 1)]
+        pltpu.make_async_copy(arrived, arrived, env_recv.at[k]).wait()
+
+        @pl.when(even)
+        def _():
+            place_right(first, last)
+
+        @pl.when(jnp.logical_not(even))
+        def _():
+            place_left(first, last)
+
+    receive(0)
     for copy in start_halo:
         copy.wait_recv()
     for k in range(3):
         sources[k * BLK : (k + 1) * BLK, :] = halo[0, k]
-    total = None
     for k, (first, last) in enumerate(CHUNKS):
-        arrived = raw.at[1 - parity, env_rows(k, 1)]
-        pltpu.make_async_copy(arrived, arrived, env_recv.at[k]).wait()
-
-        @pl.when(even)
-        def _():
-            place_right(first, last)
-
-        @pl.when(jnp.logical_not(even))
-        def _():
-            place_left(first, last)
-
+        if k:
+            receive(k)
         if k:
             image[...] += channels(first, last)
         else:
@@ -372,7 +389,7 @@
         lowest = 0.5 * (energy + curvature) - jnp.sqrt(x * x + coupling * coupling)
         return cosine, sine, lowest
 
-    def kappa_of(square):
+    def kappa_of(unit, square):
         return unit / jnp.sqrt(unit * unit * square + EPSILON)
 
     def own(row):
@@ -391,29 +408,34 @@
     for k in (0, 2):
         field = halo[1, k].astype(F32) - scaled * halo[0, k].astype(F32)
         sources[k * BLK : (k + 1) * BLK, :] = field.astype(BF16)
-    sums = {}
+    found = {}
 
     def read_first():
-        sums[0] = sum_finish(0)
-
-    unmix(channels(0, CHAN, read_first))
-    energy_now = scalar(sums[0], 0)
-    square = scalar(sums[0], 1)
-    unit = jnp.sqrt(square + EPSILON)
-    inverse = 1.0 / unit
-    t = (vec_t[...] + (quotient - energy_now) * vec_im[...]) * inverse
+        totals = sum_finish(0)
+        energy = scalar(totals, 0)
+        square = scalar(totals, 1)
+        unit = jnp.sqrt(square + EPSILON)
+        inverse = 1.0 / unit
+        im = vec_im[...]
+        q = (im - energy * start_buf[...]) * inverse
+        vec_q[...] = q
+        im_buf[...] = ((quotient - energy) * inverse) * im
+        rest = square + energy * (energy * scalar(totals, 2) - 2.0 * energy)
+        floor = 0.5 * share * jnp.maximum(rest * inverse * inverse, 1e-6)
+        found[0] = energy, unit, inverse, floor, partial(q, q), partial(q, im)
+
+    unmix(channels(0, CHAN, read_first, 5))
+    energy_now, unit, inverse, floor, part_qq, part_qi = found[0]
+    t = vec_t[...] * inverse + im_buf[...]
     vec_t[...] = t
     halo[2, 1] = t.astype(BF16)
     for copy in halos[1]:
         copy.start()
-    q = (vec_im[...] - energy_now * start_buf[...]) * inverse
-    vec_q[...] = q
-
-    row_sums = dots([(q, q), (q, vec_im[...]), (q, vec_t[...]), (start_buf[...], vec_t[...])])
+
+    t = vec_t[...]
+    row_sums = packed([part_qq, part_qi, partial(vec_q[...], t), partial(start_buf[...], t)])
     sum_start(1, row_sums)
     local = own(row_sums)
-    rest = square + energy_now * (energy_now * scalar(sums[0], 2) - 2.0 * energy_now)
-    floor = 0.5 * share * jnp.maximum(rest * inverse * inverse, 1e-6)
     along_q = scalar(local, 2) / jnp.maximum(scalar(local, 0), floor)
     along_psi = scalar(local, 3) / weight
     sources[BLK : 2 * BLK, :] = (vec_t[...] - along_q * vec_q[...] - along_psi * start_buf[...]).astype(BF16)
@@ -426,32 +448,32 @@
         sources[k * BLK : (k + 1) * BLK, :] = field.astype(BF16)
 
     def read_second():
-        sums[1] = sum_finish(1)
-
-    turned_t = channels(0, CHAN, read_second)
-    totals = sums[1]
-    kappa = kappa_of(scalar(totals, 0))
-    coupling = kappa * scalar(totals, 1)
-    curvature = kappa * kappa * scalar(totals, 2)
-    mirrored = kappa * scalar(totals, 3)
-    cosine, sine, _ = rotation(energy_now, coupling, curvature)
-    energy_next = (
-        cosine * cosine * energy_now + cosine * sine * (coupling + mirrored) + sine * sine * curvature
-    )
-    turn = sine * kappa
-    psi = cosine * start_buf[...] + turn * vec_q[...]
-    im = cosine * vec_im[...] + turn * vec_t[...]
-    known = (cosine * unit + turn * along_q) * vec_t[...] + (cosine * energy_now + turn * along_psi) * vec_im[...]
-    start_buf[...] = psi
-    q = (im - energy_next * psi) * inverse
-    vec_q[...] = q
-    vec_im[...] = known - energy_next * im
-    im_buf[...] = im
-    unmix(turned_t)
-    t = (vec_im[...] + turn * vec_t[...]) * inverse
-    sum_start(2, dots([(vec_q[...], vec_q[...]), (vec_q[...], im_buf[...]), (vec_q[...], t)]))
+        totals = sum_finish(1)
+        kappa = kappa_of(unit, scalar(totals, 0))
+        coupling = kappa * scalar(totals, 1)
+        curvature = kappa * kappa * scalar(totals, 2)
+        mirrored = kappa * scalar(totals, 3)
+        cosine, sine, _ = rotation(energy_now, coupling, curvature)
+        energy = (
+            cosine * cosine * energy_now + cosine * sine * (coupling + mirrored) + sine * sine * curvature
+        )
+        turn = sine * kappa
+        im_then, t_then = vec_im[...], vec_t[...]
+        psi = cosine * start_buf[...] + turn * vec_q[...]
+        im = cosine * im_then + turn * t_then
+        q = (im - energy * psi) * inverse
+        known = (cosine * unit + turn * along_q) * t_then + (cosine * energy_now + turn * along_psi) * im_then
+        start_buf[...] = psi
+        vec_q[...] = q
+        vec_im[...] = (known - energy * im) * inverse
+        found[1] = energy, turn * inverse, partial(q, q), partial(q, im)
+
+    unmix(channels(0, CHAN, read_second, 5))
+    energy_next, factor, part_qq, part_qi = found[1]
+    t = vec_t[...] * factor + vec_im[...]
+    sum_start(2, packed([part_qq, part_qi, partial(vec_q[...], t)]))
     totals = sum_finish(2)
-    kappa = kappa_of(scalar(totals, 0))
+    kappa = kappa_of(unit, scalar(totals, 0))
     coupling = kappa * scalar(totals, 1)
     curvature = kappa * kappa * scalar(totals, 2)
     cosine, sine, lowest = rotation(energy_next, coupling, curvature)
@@ -487,6 +509,7 @@
             pltpu.SMEM((CHAN,), jnp.int32),
             pltpu.VMEM((2 * CHAN * PAIRS, 128), BF16),
             pltpu.VMEM((2 * CHAN * PAIRS, 128), F32),
+            pltpu.VMEM((2, CHAN * PAIRS, 128), F32),
             pltpu.VMEM((2, CHAN * PAIRS, 128), BF16),
             pltpu.VMEM((CHAN * PAIRS, 128), BF16),
             pltpu.VMEM((CHAN * BLK, 3 * BLK), BF16),
@@ -496,7 +519,6 @@
             pltpu.VMEM((3 * BLK, WIDTH), BF16),
             pltpu.VMEM((3, 3, BLK, WIDTH), BF16),
             pltpu.VMEM((BLK, 128), F32),
-            pltpu.VMEM((PH // 2, BLK, 128), F32),
             pltpu.VMEM((BLK, WIDTH), F32),
             pltpu.VMEM((BLK, WIDTH), F32),
             pltpu.VMEM((BLK, WIDTH), F32),

time: 41.4 us -> 40.5 us (0.978)
  Pallas kernels: 38.8 us -> 37.9 us
    pallas_call x1, Pallas kernels: 38.8 us -> 37.9 us  [body(): pl.pallas_call(kernel, out_shape=(pltpu.VMEM((1, BLK, WIDTH), F32), pltpu...]
where the time goes in v5:
time: 40.5 us; the launch traced here: 40.4 us
  Pallas kernels  37.9 us (94%)
  between operations  1.8 us (4%)
  local copies, waits for them, and re-layouts  0.71 us (2%)
    pallas_call x1, Pallas kernels, body(): pl.pallas_call(kernel, out_shape=(pltpu.VMEM((1, BLK, WIDTH), F32), pltpu...  37.9 us

profile of v5, /device:TPU:1, one launch (start us, length us, event | category | flops | bytes accessed | tf_op | source)
XLA Modules:
  0.0 40.4 jit_solution(12850088590658972801)
XLA Ops:
  0.6 37.9 %shard_map.68 = (f32[1,64,1024]{2,1,0:T(8,128)S(1)}, f32[1,128]{1,0:T(1,128)S(1)}) custom-call(f32[1,64,1024]{2,1,0:T(8,128)} %wave_hbm.1, bf16[2176,128]{1,0:T(8,128)(2,1)} %bitcast.9, bf16[16,16,34]{2,1,0:T(8,128)(2,1)} %bitcast.10, s32[1,2]{1,0:T(1,128)} %dims_hbm.1, s32[34]{0:T(128)} %charge_hbm.1), custom_call_target="tpu_custom_call" | custom-call | tf_op jit(solution)/shard_map/pallas_call | solution.py:497
  38.5 0.7 %copy.10 = f32[1,64,1024]{2,1,0:T(8,128)} copy(f32[1,64,1024]{2,1,0:T(8,128)S(1)} %get-tuple-element.6) | data formatting | bytes 524288

commit v6 on v5

--- a/solution.py
+++ b/solution.py
@@ -19,7 +19,8 @@
 WIDTH = PH * BLK
 PAIRS = BLK // 2
 
-NEAR = tuple((0, d) for d in range(8))
+CORES = ((0, 0), (0, 1))
+RING = ((0, 0), (0, 2), (0, 4), (0, 6))
 ACROSS = ((0, 0), (0, 8), (1, 0), (1, 8))
 EVERY = tuple((h, d) for h in (0, 1) for d in range(16))
 
@@ -88,7 +89,7 @@
     below = (section, (inner + n_inner - 1) % n_inner)
     partner = at(1, 0)
 
-    peers = [partner, above, below] + [at(h, d) for h, d in NEAR[1:] + ACROSS[1:2] + ACROSS[3:]]
+    peers = [partner, above, below] + [at(h, d) for h, d in CORES[1:] + RING[1:] + ACROSS[1:2] + ACROSS[3:]]
     barrier = pltpu.get_barrier_semaphore()
     for peer in peers:
         pl.semaphore_signal(barrier, inc=1, device_id=peer, device_id_type=MESH)
@@ -262,12 +263,20 @@
         copy.start()
     for copy in env_copies[1:]:
         copy.start()
-    send_row(near_buf.at[0], NEAR, norm_row, near_send.at[0], near_recv.at[0])
+    send_row(near_buf.at[0], CORES, norm_row, near_send.at[0], near_recv.at[0])
 
     zero = jnp.zeros((2 * BLK, 128), BF16)
     for a in range(CHAN):
         rsel[a, 0:128, 128:256] = zero
         rsel[a, 128:256, 0:128] = zero
+
+    def four(k):
+        part = [near_buf[k, n : n + 1, :] for n in range(4)]
+        return (part[0] + part[1]) + (part[2] + part[3])
+
+    await_rows(near_buf.at[0], CORES, near_recv.at[0])
+    norm_row = near_buf[0, 0:1, :] + near_buf[0, 1:2, :]
+    send_row(near_buf.at[1], RING, norm_row, near_send.at[1], near_recv.at[1])
 
     def iota(shape, axis):
         return lax.broadcasted_iota(jnp.int32, shape, axis)
@@ -324,9 +333,8 @@
     def _():
         place_right(0, CHAN)
 
-    await_rows(near_buf.at[0], NEAR, near_recv.at[0])
-    norm_row = total_rows(near_buf[0])[0:1, :]
-    send_row(near_buf.at[1], ACROSS, norm_row, near_send.at[1], near_recv.at[1])
+    await_rows(near_buf.at[1], RING, near_recv.at[1])
+    send_row(near_buf.at[2], ACROSS, four(1), near_send.at[2], near_recv.at[2])
 
     def receive(k):
         first, last = CHUNKS[k]
@@ -354,9 +362,8 @@
         else:
             image[...] = channels(first, last)
 
-    await_rows(near_buf.at[1], ACROSS, near_recv.at[1])
-    part = [near_buf[1, k : k + 1, :] for k in range(4)]
-    norm_row = (part[0] + part[1]) + (part[2] + part[3])
+    await_rows(near_buf.at[2], ACROSS, near_recv.at[2])
+    norm_row = four(2)
     norm = jnp.sum(jnp.where(lane8[0:1] < 32, norm_row, 0.0), axis=1, keepdims=True) * (1.0 / entries)
     scale = 1.0 / jnp.sqrt(norm + EPSILON)
     unmix(image[...])
@@ -480,8 +487,8 @@
     psi_ref[0] = cosine * start_buf[...] + (sine * kappa) * vec_q[...]
     energy_ref[...] = jnp.broadcast_to(lowest, (1, 128))
 
-    await_rows(near_buf.at[0], NEAR, near_send.at[0])
-    await_rows(near_buf.at[1], ACROSS, near_send.at[1])
+    for k, group in enumerate((CORES, RING, ACROSS)):
+        await_rows(near_buf.at[k], group, near_send.at[k])
     for k in range(3):
         await_rows(exchange.at[k], EVERY, red_send.at[k])
     for copies in [env_copies, start_halo] + halos:
@@ -524,7 +531,7 @@
             pltpu.VMEM((BLK, WIDTH), F32),
             pltpu.VMEM((BLK, WIDTH), F32),
             pltpu.VMEM((BLK, WIDTH), F32),
-            pltpu.VMEM((2, 8, 128), F32),
+            pltpu.VMEM((3, 8, 128), F32),
             pltpu.VMEM((3, 32, 128), F32),
             pltpu.SemaphoreType.DMA((4,)),
             pltpu.SemaphoreType.DMA((len(CHUNKS),)),
@@ -532,8 +539,8 @@
             pltpu.SemaphoreType.DMA((len(CHUNKS),)),
             pltpu.SemaphoreType.DMA((3, 2)),
             pltpu.SemaphoreType.DMA((3, 2)),
-            pltpu.SemaphoreType.DMA((2,)),
-            pltpu.SemaphoreType.DMA((2,)),
+            pltpu.SemaphoreType.DMA((3,)),
+            pltpu.SemaphoreType.DMA((3,)),
             pltpu.SemaphoreType.DMA((3,)),
             pltpu.SemaphoreType.DMA((3,)),
         ],

time: 40.5 us -> 40.5 us (level)
  no operation moved by 1% of the time
where the time goes in v6:
time: 40.5 us; the launch traced here: 40.4 us
  Pallas kernels  37.9 us (94%)
  between operations  1.8 us (4%)
  local copies, waits for them, and re-layouts  0.71 us (2%)
    pallas_call x1, Pallas kernels, body(): pl.pallas_call(kernel, out_shape=(pltpu.VMEM((1, BLK, WIDTH), F32), pltpu...  37.9 us

profile of v6, /device:TPU:1, one launch (start us, length us, event | category | flops | bytes accessed | tf_op | source)
XLA Modules:
  0.0 40.4 jit_solution(758503637840153502)
XLA Ops:
  0.6 37.9 %shard_map.68 = (f32[1,64,1024]{2,1,0:T(8,128)S(1)}, f32[1,128]{1,0:T(1,128)S(1)}) custom-call(f32[1,64,1024]{2,1,0:T(8,128)} %wave_hbm.1, bf16[2176,128]{1,0:T(8,128)(2,1)} %bitcast.9, bf16[16,16,34]{2,1,0:T(8,128)(2,1)} %bitcast.10, s32[1,2]{1,0:T(1,128)} %dims_hbm.1, s32[34]{0:T(128)} %charge_hbm.1), custom_call_target="tpu_custom_call" | custom-call | tf_op jit(solution)/shard_map/pallas_call | solution.py:504
  38.5 0.7 %copy.10 = f32[1,64,1024]{2,1,0:T(8,128)} copy(f32[1,64,1024]{2,1,0:T(8,128)S(1)} %get-tuple-element.6) | data formatting | bytes 524288
